TPU v7x, 32 devices: a whole 2x2x4 slice. The times are simulated.
32 devices in a mesh: section: 2 (over x), tensor: 4 (over y, core), dp: 4 (over z).
Axes of the slice: x: 2, y: 2, z: 4, core: 2. Of those that a mesh axis runs over, the one named last changes fastest.
Arguments:
- tokens: bfloat16 [3, 512, 768], P(None, 'dp'), may hold values from -3 to 3
- block_order: int32 [3, 4], replicated, may hold values from 0 to 3, each once within a row
- ln_gain: float32 [2, 2, 768], P('section'), may hold values from 0.5 to 1.5
- ln_bias: float32 [2, 2, 768], P('section'), may hold values from -0.75 to 0.75
- qkv_weight: bfloat16 [2, 768, 3, 768], P('section', None, None, 'tensor'), may hold values from -0.12597656 to 0.12597656
- qv_bias: float32 [2, 2, 768], P('section', None, 'tensor'), may hold values from -0.75 to 0.75
- out_weight: bfloat16 [2, 768, 768], P('section', 'tensor'), may hold values from -0.3125 to 0.3125
- out_bias: float32 [2, 768], P('section'), may hold values from -0.75 to 0.75
- fc_weight: bfloat16 [2, 768, 3072], P('section', None, 'tensor'), may hold values from -0.21875 to 0.21875
- fc_bias: float32 [2, 3072], P('section', 'tensor'), may hold values from -0.75 to 0.75
- proj_weight: bfloat16 [2, 3072, 768], P('section', 'tensor'), may hold values from -0.109375 to 0.109375
- proj_bias: float32 [2, 768], P('section'), may hold values from -0.75 to 0.75
- cotangent: bfloat16 [3, 512, 768], P(None, 'dp'), may hold values from -3 to 3
Outputs:
- section_out: bfloat16 [2, 3, 512, 768], P('section', None, 'dp')
- section_grad: float32 [2, 3, 512, 768], P('section', None, 'dp')
- grad_ln_gain: float32 [2, 2, 768], P('section')
- grad_ln_bias: float32 [2, 2, 768], P('section')
- grad_qkv_weight: float32 [2, 768, 3, 768], P('section', None, None, 'tensor')
- grad_qv_bias: float32 [2, 2, 768], P('section', None, 'tensor')
- grad_out_weight: float32 [2, 768, 768], P('section', 'tensor')
- grad_out_bias: float32 [2, 768], P('section')
- grad_fc_weight: float32 [2, 768, 3072], P('section', None, 'tensor')
- grad_fc_bias: float32 [2, 3072], P('section', 'tensor')
- grad_proj_weight: float32 [2, 3072, 768], P('section', 'tensor')
- grad_proj_bias: float32 [2, 768], P('section')
Inputs may be any that keep to these rules, and one draw needn't show every extreme that they name: Each row is a permutation: index j of dp holds the positions from 128 * block_order[m, j] on.
All inputs are finite; a program needn't handle non-finite values.
Results may differ from a plain program's by a relative error of at most 0.025.
The roundings to bfloat16 on the way count: a program that leaves them out, or rounds other values in their place, can miss the bound.
Values may be sent and summed in bfloat16 or wider, within the bound.
A program may use at most 128 MiB of HBM per device.

v0:
```python
import math

import jax
import jax.numpy as jnp
from jax import lax
from jax.sharding import PartitionSpec as P

HEAD = 64


EPSILON = 1e-05
MASKED = -1e30
GELU_RATE = 0.7978845608028654
GELU_CUBE = 0.044715


def passed_along(block, axis, distance):
    devices = range(lax.axis_size(axis))
    route = [(i - distance, i) for i in devices if i - distance in devices]
    return lax.ppermute(block, axis, route)


def layer_norm(values, gains, biases):
    average = jnp.mean(values, axis=-1, keepdims=True)
    centered = values - average
    spread = jnp.mean(centered * centered, axis=-1, keepdims=True)
    return centered * lax.rsqrt(spread + EPSILON) * gains + biases


def gelu_tanh(values):
    return (
        0.5 * values * (1.0 + jnp.tanh(GELU_RATE * (values + GELU_CUBE * values * values * values)))
    )


def contract_rows(left, right):
    return lax.dot_general(
        left, right, (((0,), (0,)), ((), ())), preferred_element_type=jnp.float32
    )


def contract_cols(left, right):
    return lax.dot_general(
        left, right, (((1,), (1,)), ((), ())), preferred_element_type=jnp.float32
    )


def key_positions(row_order, key_count, shard_rows):
    row_index = jnp.arange(key_count, dtype=jnp.int32)
    owners = row_index // shard_rows
    owner_table = (
        owners[:, None] == jnp.arange(row_order.shape[0], dtype=jnp.int32)[None, :]
    ).astype(jnp.int32)
    return jnp.sum(owner_table * row_order[None, :], axis=1) * shard_rows + row_index % shard_rows


def score_maker(query, query_pos, row_order, shard_rows):
    query_rows = query.shape[0]
    head_count = query.shape[1] // HEAD
    queries = query.reshape(query_rows, head_count, HEAD)
    score_scale = 1.0 / math.sqrt(HEAD)

    def scores_for(piece_keys, begin_row):
        key_count = piece_keys.shape[0]
        key_pos = key_positions(row_order, key_count, shard_rows)
        key_heads = piece_keys.reshape(key_count, head_count, HEAD)
        scores = (
            jnp.einsum("qhe,khe->hqk", queries, key_heads, preferred_element_type=jnp.float32)
            * score_scale
        )
        allowed = (query_pos[:, None] >= key_pos[None, :])[None, :, :]
        return (scores, allowed, key_heads)

    return (scores_for, queries, head_count)


def attend_forward(query, keys, values, query_pos, row_order, shard_rows):
    scores_for, queries, head_count = score_maker(query, query_pos, row_order, shard_rows)
    query_rows = query.shape[0]
    row_peak = jnp.full((head_count, query_rows), MASKED, jnp.float32)
    scores, allowed, key_heads = scores_for(
        lax.all_gather(keys, "dp", axis=0, tiled=True), jnp.int32(0)
    )
    new_peak = jnp.maximum(row_peak, jnp.max(jnp.where(allowed, scores, MASKED), axis=-1))
    fresh = jnp.sum(jnp.where(allowed, jnp.exp(scores - new_peak[:, :, None]), 0.0), axis=-1)
    log_total = new_peak + jnp.log(fresh)
    pieces = (
        lax.all_gather(keys, "dp", axis=0, tiled=True),
        lax.all_gather(values, "dp", axis=0, tiled=True),
    )
    scores, allowed, key_heads = scores_for(pieces[0], jnp.int32(0))
    softmax_low = jnp.where(allowed, jnp.exp(scores - log_total[:, :, None]), 0.0).astype(
        jnp.bfloat16
    )
    value_heads = pieces[1].reshape(pieces[1].shape[0], head_count, HEAD)
    attended = jnp.einsum(
        "hqk,khe->qhe", softmax_low, value_heads, preferred_element_type=jnp.float32
    )
    return (attended.reshape(query_rows, head_count * HEAD), log_total, None)


def attend_backward(
    query, keys, values, grad_attended, log_total, query_pos, row_order, shard_rows
):
    scores_for, queries, head_count = score_maker(query, query_pos, row_order, shard_rows)
    query_rows = query.shape[0]
    score_scale = 1.0 / math.sqrt(HEAD)
    grad_heads = grad_attended.reshape(query_rows, head_count, HEAD)

    def softmax_parts(pieces, begin_row):
        scores, allowed, key_heads = scores_for(pieces[0], begin_row)
        softmax = jnp.where(allowed, jnp.exp(scores - log_total[:, :, None]), 0.0)
        value_heads = pieces[1].reshape(pieces[1].shape[0], head_count, HEAD)
        grad_softmax = jnp.einsum(
            "qhe,khe->hqk", grad_heads, value_heads, preferred_element_type=jnp.float32
        )
        return (softmax, grad_softmax, key_heads)

    softmax, grad_softmax, key_heads = softmax_parts(
        (
            lax.all_gather(keys, "dp", axis=0, tiled=True),
            lax.all_gather(values, "dp", axis=0, tiled=True),
        ),
        jnp.int32(0),
    )
    delta = jnp.sum(softmax * grad_softmax, axis=-1)
    local_width = head_count * HEAD
    pieces = (
        lax.all_gather(keys, "dp", axis=0, tiled=True),
        lax.all_gather(values, "dp", axis=0, tiled=True),
    )
    softmax, grad_softmax, key_heads = softmax_parts(pieces, jnp.int32(0))
    grad_scores = (softmax * (grad_softmax - delta[:, :, None])).astype(jnp.bfloat16)
    grad_query = (
        jnp.einsum("hqk,khe->qhe", grad_scores, key_heads, preferred_element_type=jnp.float32)
        * score_scale
    )
    grad_keys = (
        jnp.einsum("hqk,qhe->khe", grad_scores, queries, preferred_element_type=jnp.float32)
        * score_scale
    )
    grad_values = jnp.einsum(
        "hqk,qhe->khe", softmax.astype(jnp.bfloat16), grad_heads, preferred_element_type=jnp.float32
    )
    key_count = pieces[0].shape[0]
    piece_terms = jnp.concatenate(
        [grad_keys.reshape(key_count, -1), grad_values.reshape(key_count, -1)], axis=1
    )
    folded = (grad_query, piece_terms)
    grad_query, key_terms = folded
    key_grads = lax.psum_scatter(key_terms, "dp", scatter_dimension=0, tiled=True)
    grad_keys = key_grads[:, :local_width]
    grad_values = key_grads[:, local_width:]
    return (
        grad_query.reshape(query_rows, local_width).astype(jnp.bfloat16),
        grad_keys.astype(jnp.bfloat16),
        grad_values.astype(jnp.bfloat16),
    )


def layer_forward(inputs, query_pos, row_order, params):
    (
        gains,
        biases,
        qkv_weight,
        qv_bias,
        out_weight,
        out_bias,
        fc_weight,
        fc_bias,
        proj_weight,
        proj_bias,
    ) = params
    shard_rows = inputs.shape[0]
    local_width = qkv_weight.shape[2]
    normed = layer_norm(inputs, gains[0], biases[0]).astype(jnp.bfloat16)
    projected = jnp.dot(
        normed,
        qkv_weight.reshape(qkv_weight.shape[0], 3 * local_width),
        preferred_element_type=jnp.float32,
    )
    query = (projected[:, :local_width] + qv_bias[0]).astype(jnp.bfloat16)
    keys = projected[:, local_width : 2 * local_width].astype(jnp.bfloat16)
    values = (projected[:, 2 * local_width :] + qv_bias[1]).astype(jnp.bfloat16)
    attended, log_total, gathered = attend_forward(
        query, keys, values, query_pos, row_order, shard_rows
    )
    attended = attended.astype(jnp.bfloat16)
    middle = (
        inputs
        + lax.psum(jnp.dot(attended, out_weight, preferred_element_type=jnp.float32), "tensor")
        + out_bias
    )
    normed_mid = layer_norm(middle, gains[1], biases[1]).astype(jnp.bfloat16)
    hidden_pre = jnp.dot(normed_mid, fc_weight, preferred_element_type=jnp.float32) + fc_bias
    active = gelu_tanh(hidden_pre).astype(jnp.bfloat16)
    output = (
        middle
        + lax.psum(jnp.dot(active, proj_weight, preferred_element_type=jnp.float32), "tensor")
        + proj_bias
    )
    saved_state = (
        inputs,
        query_pos,
        row_order,
        normed,
        query,
        keys,
        values,
        log_total,
        attended,
        middle,
        normed_mid,
        hidden_pre,
        active,
        gathered,
    )
    return (output, saved_state)


def layer_backward(grad_output, saved_state, params):
    (
        gains,
        biases,
        qkv_weight,
        qv_bias,
        out_weight,
        out_bias,
        fc_weight,
        fc_bias,
        proj_weight,
        proj_bias,
    ) = params
    (
        inputs,
        query_pos,
        row_order,
        normed,
        query,
        keys,
        values,
        log_total,
        attended,
        middle,
        normed_mid,
        hidden_pre,
        active,
        gathered,
    ) = saved_state
    grad_low = grad_output.astype(jnp.bfloat16)
    grad_proj_bias = jnp.sum(grad_output, axis=0)
    grad_proj_weight = contract_rows(active, grad_low)
    grad_active = contract_cols(grad_low, proj_weight)
    grad_pre = jax.vjp(gelu_tanh, hidden_pre)[1](grad_active)[0].astype(jnp.bfloat16)
    grad_fc_bias = jnp.sum(grad_pre.astype(jnp.float32), axis=0)
    grad_fc_weight = contract_rows(normed_mid, grad_pre)
    grad_normed_mid = lax.psum(contract_cols(grad_pre, fc_weight), "tensor")
    grad_middle_norm, grad_gain_mid, grad_bias_mid = jax.vjp(
        layer_norm, middle, gains[1], biases[1]
    )[1](grad_normed_mid)
    grad_middle = grad_output + grad_middle_norm
    middle_low = grad_middle.astype(jnp.bfloat16)
    grad_out_bias = jnp.sum(grad_middle, axis=0)
    grad_out_weight = contract_rows(attended, middle_low)
    grad_attended = contract_cols(middle_low, out_weight).astype(jnp.bfloat16)
    grad_query, grad_keys, grad_values = attend_backward(
        query, keys, values, grad_attended, log_total, query_pos, row_order, inputs.shape[0]
    )
    grad_projected = jnp.concatenate([grad_query, grad_keys, grad_values], axis=1)
    qkv_flat = qkv_weight.reshape(qkv_weight.shape[0], -1)
    grad_qkv_weight = contract_rows(normed, grad_projected).reshape(qkv_weight.shape)
    grad_qv_bias = jnp.stack(
        [
            jnp.sum(grad_query.astype(jnp.float32), axis=0),
            jnp.sum(grad_values.astype(jnp.float32), axis=0),
        ]
    )
    grad_normed = lax.psum(contract_cols(grad_projected, qkv_flat), "tensor")
    grad_input_norm, grad_gain_in, grad_bias_in = jax.vjp(layer_norm, inputs, gains[0], biases[0])[
        1
    ](grad_normed)
    grad_input = grad_middle + grad_input_norm
    grads = (
        jnp.stack([grad_gain_in, grad_gain_mid]),
        jnp.stack([grad_bias_in, grad_bias_mid]),
        grad_qkv_weight,
        grad_qv_bias,
        grad_out_weight,
        grad_out_bias,
        grad_fc_weight,
        grad_fc_bias,
        grad_proj_weight,
        grad_proj_bias,
    )
    return (grad_input, grads)


def per_device(
    tokens,
    block_order,
    ln_gain,
    ln_bias,
    qkv_weight,
    qv_bias,
    out_weight,
    out_bias,
    fc_weight,
    fc_bias,
    proj_weight,
    proj_bias,
    cotangent,
):
    micro_count, shard_rows, model_width = tokens.shape
    is_first = lax.axis_index("section") == 0
    dp_index = lax.axis_index("dp")
    params = (
        ln_gain[0],
        ln_bias[0],
        qkv_weight[0],
        qv_bias[0],
        out_weight[0],
        out_bias[0],
        fc_weight[0],
        fc_bias[0],
        proj_weight[0],
        proj_bias[0],
    )
    row_offsets = jnp.arange(shard_rows, dtype=jnp.int32)
    received = jnp.zeros((shard_rows, model_width), jnp.float32)
    saved_ticks = []
    out_ticks = []
    for step_index in range(micro_count + 1):
        feed = tokens[min(step_index, micro_count - 1)].astype(jnp.float32)
        inputs = jnp.where(is_first, feed, received)
        row_order = jnp.where(
            is_first,
            block_order[min(step_index, micro_count - 1)],
            block_order[max(step_index - 1, 0)],
        )
        query_pos = row_order[dp_index] * shard_rows + row_offsets
        output, saved_state = layer_forward(inputs, query_pos, row_order, params)
        output_low = output.astype(jnp.bfloat16)
        out_ticks.append(output_low)
        saved_ticks.append(saved_state)
        if step_index < micro_count:
            received = passed_along(output_low, "section", 1).astype(jnp.float32)
    received_grad = jnp.zeros((shard_rows, model_width), jnp.float32)
    grad_ticks = []
    totals = None
    for step_index in range(micro_count + 1):
        saved_state = jax.tree.map(
            lambda early, late: jnp.where(is_first, early, late),
            saved_ticks[max(step_index - 1, 0)],
            saved_ticks[min(step_index + 1, micro_count)],
        )
        seed_grad = cotangent[min(step_index, micro_count - 1)].astype(jnp.float32)
        grad_output = jnp.where(is_first, received_grad, seed_grad)
        grad_input, grads = layer_backward(grad_output, saved_state, params)
        is_valid = jnp.where(is_first, step_index >= 1, step_index < micro_count).astype(
            jnp.float32
        )
        scaled = tuple((is_valid * member for member in grads))
        totals = (
            scaled
            if totals is None
            else tuple((earlier + latest for earlier, latest in zip(totals, scaled)))
        )
        grad_ticks.append(grad_input)
        if step_index < micro_count:
            received_grad = passed_along(grad_input.astype(jnp.bfloat16), "section", -1).astype(
                jnp.float32
            )
    summed = lax.psum(totals, "dp")
    section_out = jnp.stack(
        [
            jnp.where(is_first, out_ticks[batch_index], out_ticks[batch_index + 1])
            for batch_index in range(micro_count)
        ]
    )[None]
    section_grad = jnp.stack(
        [
            jnp.where(is_first, grad_ticks[batch_index + 1], grad_ticks[batch_index])
            for batch_index in range(micro_count)
        ]
    )[None]
    return (section_out, section_grad) + tuple((member[None] for member in summed))


def solution(mesh):
    return jax.shard_map(
        per_device,
        mesh=mesh,
        in_specs=(
            P(None, "dp", None),
            P(),
            P("section", None, None),
            P("section", None, None),
            P("section", None, None, "tensor"),
            P("section", None, "tensor"),
            P("section", "tensor", None),
            P("section", None),
            P("section", None, "tensor"),
            P("section", "tensor"),
            P("section", "tensor", None),
            P("section", None),
            P(None, "dp", None),
        ),
        out_specs=(
            P("section", None, "dp", None),
            P("section", None, "dp", None),
            P("section", None, None),
            P("section", None, None),
            P("section", None, None, "tensor"),
            P("section", None, "tensor"),
            P("section", "tensor", None),
            P("section", None),
            P("section", None, "tensor"),
            P("section", "tensor"),
            P("section", "tensor", None),
            P("section", None),
        ),
        check_vma=False,
    )
```

profile of v0, /device:TPU:0, one launch (start us, length us, event | category | flops | bytes accessed | tf_op | source)
XLA Modules:
  0.0 1044.9 jit_solution(8281543648847936734)
XLA Ops:
  16.4 14.2 %all_gather.61 = bf16[512,192]{0,1:T(8,128)(2,1)S(1)} all-gather(bf16[128,192]{0,1:T(8,128)(2,1)S(1)} %slice.357), channel_id=1, replica_groups=mesh['section'=2,'tensor'=4,'dp'=4] {'dp'}, dimensions={0}, use_global_device_ids=true | all-gather | bytes 245760 | tf_op jit(solution)/shard_map/all_gather | solution.py:88
  30.8 12.7 %all_gather.60 = bf16[512,192]{0,1:T(8,128)(2,1)S(1)} all-gather(bf16[128,192]{0,1:T(8,128)(2,1)S(1)} %get-tuple-element.170), channel_id=1, replica_groups=mesh['section'=2,'tensor'=4,'dp'=4] {'dp'}, dimensions={0}, use_global_device_ids=true | all-gather | bytes 245760 | tf_op jit(solution)/shard_map/all_gather | solution.py:89
  56.7 21.0 %all-reduce.20.cloned.1.call-done = f32[128,768]{1,0:T(8,128)} async-done(((f32[128,768]{1,0:T(8,128)}), f32[128,768]{1,0:T(8,128)}) %all-reduce.20.cloned.1.call-update) | async-done | bytes 393232 | tf_op jit(solution)/shard_map/psum | solution.py:191
  82.0 32.1 %all-reduce.22.cloned.1.call-done = f32[128,768]{1,0:T(8,128)} async-done(((f32[128,768]{1,0:T(8,128)}), f32[128,768]{1,0:T(8,128)}) %all-reduce.22.cloned.1.call-update) | async-done | bytes 393232 | tf_op jit(solution)/shard_map/psum | solution.py:199
  115.3 3.5 collective-permute-start
  125.7 13.6 %all_gather.68 = bf16[512,192]{0,1:T(8,128)(2,1)} all-gather(bf16[128,192]{0,1:T(8,128)(2,1)S(1)} %get-tuple-element.137), channel_id=1, replica_groups=mesh['section'=2,'tensor'=4,'dp'=4] {'dp'}, dimensions={0}, use_global_device_ids=true | all-gather | bytes 245760 | tf_op jit(solution)/shard_map/all_gather | solution.py:129
  139.2 13.5 %all_gather.69 = bf16[512,192]{0,1:T(8,128)(2,1)} all-gather(bf16[128,192]{0,1:T(8,128)(2,1)S(1)} %get-tuple-element.167), channel_id=1, replica_groups=mesh['section'=2,'tensor'=4,'dp'=4] {'dp'}, dimensions={0}, use_global_device_ids=true | all-gather | bytes 245760 | tf_op jit(solution)/shard_map/all_gather | solution.py:130
  152.7 13.0 %all_gather.63 = bf16[512,192]{0,1:T(8,128)(2,1)S(1)} all-gather(bf16[128,192]{0,1:T(8,128)(2,1)S(1)} %get-tuple-element.138), channel_id=1, replica_groups=mesh['section'=2,'tensor'=4,'dp'=4] {'dp'}, dimensions={0}, use_global_device_ids=true | all-gather | bytes 245760 | tf_op jit(solution)/shard_map/all_gather | solution.py:88
  165.7 12.5 %all_gather.62 = bf16[512,192]{0,1:T(8,128)(2,1)S(1)} all-gather(bf16[128,192]{0,1:T(8,128)(2,1)S(1)} %get-tuple-element.168), channel_id=1, replica_groups=mesh['section'=2,'tensor'=4,'dp'=4] {'dp'}, dimensions={0}, use_global_device_ids=true | all-gather | bytes 245760 | tf_op jit(solution)/shard_map/all_gather | solution.py:89
  181.9 30.9 %all-reduce.24.cloned.1.call-done = f32[128,768]{1,0:T(8,128)} async-done(((f32[128,768]{1,0:T(8,128)}), f32[128,768]{1,0:T(8,128)}) %all-reduce.24.cloned.1.call-update) | async-done | bytes 393232 | tf_op jit(solution)/shard_map/psum | solution.py:191
  222.8 3.0 fusion.164
  225.7 31.9 %all-reduce.42.cloned.1.call-done = (f32[128,768]{1,0:T(8,128)}, f32[128,768]{1,0:T(8,128)}) async-done(((f32[128,768]{1,0:T(8,128)}, f32[128,768]{1,0:T(8,128)}), (f32[128,768]{1,0:T(8,128)}, f32[128,768]{1,0:T(8,128)})) %all-reduce.42.cloned.1.call-update) | async-done | bytes 786448 | tf_op jit(solution)/shard_map/psum | solution.py:199
  263.8 4.0 collective-permute-start.1
  271.1 2.6 convert_reduce_fusion.11
  280.2 15.6 %all_gather.65 = bf16[512,192]{0,1:T(8,128)(2,1)S(1)} all-gather(bf16[128,192]{0,1:T(8,128)(2,1)S(1)} %get-tuple-element.121), channel_id=1, replica_groups=mesh['section'=2,'tensor'=4,'dp'=4] {'dp'}, dimensions={0}, use_global_device_ids=true | all-gather | bytes 245760 | tf_op jit(solution)/shard_map/all_gather | solution.py:88
  295.8 12.9 %all_gather.64 = bf16[512,192]{0,1:T(8,128)(2,1)S(1)} all-gather(bf16[128,192]{0,1:T(8,128)(2,1)S(1)} %get-tuple-element.164), channel_id=1, replica_groups=mesh['section'=2,'tensor'=4,'dp'=4] {'dp'}, dimensions={0}, use_global_device_ids=true | all-gather | bytes 245760 | tf_op jit(solution)/shard_map/all_gather | solution.py:89
  315.9 13.4 %all_gather.70 = bf16[512,192]{0,1:T(8,128)(2,1)} all-gather(bf16[128,192]{0,1:T(8,128)(2,1)} %get-tuple-element.120), channel_id=1, replica_groups=mesh['section'=2,'tensor'=4,'dp'=4] {'dp'}, dimensions={0}, use_global_device_ids=true | all-gather | bytes 245760 | tf_op jit(solution)/shard_map/all_gather | solution.py:129
  329.3 13.1 %all_gather.71 = bf16[512,192]{0,1:T(8,128)(2,1)} all-gather(bf16[128,192]{0,1:T(8,128)(2,1)S(1)} %copy-done.136), channel_id=1, replica_groups=mesh['section'=2,'tensor'=4,'dp'=4] {'dp'}, dimensions={0}, use_global_device_ids=true | all-gather | bytes 245760 | tf_op jit(solution)/shard_map/all_gather | solution.py:130
  342.4 3.0 fusion.171
  364.8 3.1 fusion.162
  367.9 3.2 fusion.156
  371.1 30.5 %all-reduce.38.cloned.1.call-done = (f32[128,768]{1,0:T(8,128)}, f32[128,768]{1,0:T(8,128)}) async-done(((f32[128,768]{1,0:T(8,128)}, f32[128,768]{1,0:T(8,128)}), (f32[128,768]{1,0:T(8,128)}, f32[128,768]{1,0:T(8,128)})) %all-reduce.38.cloned.1.call-update) | async-done | bytes 786448 | tf_op jit(solution)/shard_map/psum | solution.py:199
  408.0 4.0 collective-permute-start.2
  415.1 2.6 convert_reduce_fusion.9
  418.9 2.9 fusion.293
  424.4 15.6 %all_gather.67 = bf16[512,192]{0,1:T(8,128)(2,1)S(1)} all-gather(bf16[128,192]{0,1:T(8,128)(2,1)S(1)} %get-tuple-element.96), channel_id=1, replica_groups=mesh['section'=2,'tensor'=4,'dp'=4] {'dp'}, dimensions={0}, use_global_device_ids=true | all-gather | bytes 245760 | tf_op jit(solution)/shard_map/all_gather | solution.py:88
  440.0 12.9 %all_gather.66 = bf16[512,192]{0,1:T(8,128)(2,1)S(1)} all-gather(bf16[128,192]{0,1:T(8,128)(2,1)S(1)} %get-tuple-element.160), channel_id=1, replica_groups=mesh['section'=2,'tensor'=4,'dp'=4] {'dp'}, dimensions={0}, use_global_device_ids=true | all-gather | bytes 245760 | tf_op jit(solution)/shard_map/all_gather | solution.py:89
  453.5 13.1 %all_gather.74 = bf16[512,192]{0,1:T(8,128)(2,1)} all-gather(bf16[128,192]{0,1:T(8,128)(2,1)S(1)} %get-tuple-element.95), channel_id=1, replica_groups=mesh['section'=2,'tensor'=4,'dp'=4] {'dp'}, dimensions={0}, use_global_device_ids=true | all-gather | bytes 245760 | tf_op jit(solution)/shard_map/all_gather | solution.py:129
  466.6 13.1 %all_gather.73 = bf16[512,192]{0,1:T(8,128)(2,1)} all-gather(bf16[128,192]{0,1:T(8,128)(2,1)S(1)} %broadcast_select_fusion.11), channel_id=1, replica_groups=mesh['section'=2,'tensor'=4,'dp'=4] {'dp'}, dimensions={0}, use_global_device_ids=true | all-gather | bytes 245760 | tf_op jit(solution)/shard_map/all_gather | solution.py:130
  480.4 13.4 %all_gather.72 = bf16[512,192]{0,1:T(8,128)(2,1)} all-gather(bf16[128,192]{0,1:T(8,128)(2,1)S(1)} %broadcast_select_fusion.13), channel_id=1, replica_groups=mesh['section'=2,'tensor'=4,'dp'=4] {'dp'}, dimensions={0}, use_global_device_ids=true | all-gather | bytes 245760 | tf_op jit(solution)/shard_map/all_gather | solution.py:129
  501.8 13.4 %all_gather.75 = bf16[512,192]{0,1:T(8,128)(2,1)} all-gather(bf16[128,192]{0,1:T(8,128)(2,1)} %get-tuple-element.159), channel_id=1, replica_groups=mesh['section'=2,'tensor'=4,'dp'=4] {'dp'}, dimensions={0}, use_global_device_ids=true | all-gather | bytes 245760 | tf_op jit(solution)/shard_map/all_gather | solution.py:130
  519.0 15.0 %all-reduce.36.cloned.1.call-done = (f32[128,768]{1,0:T(8,128)}, f32[128,768]{1,0:T(8,128)}) async-done(((f32[128,768]{1,0:T(8,128)}, f32[128,768]{1,0:T(8,128)}), (f32[128,768]{1,0:T(8,128)}, f32[128,768]{1,0:T(8,128)})) %all-reduce.36.cloned.1.call-update) | async-done | bytes 786448 | tf_op jit(solution)/shard_map/psum | solution.py:191
  550.3 5.1 collective-permute-done.4
  561.0 31.3 %all-reduce.26.cloned.1.call-done = f32[128,768]{1,0:T(8,128)} async-done(((f32[128,768]{1,0:T(8,128)}), f32[128,768]{1,0:T(8,128)}) %all-reduce.26.cloned.1.call-update) | async-done | bytes 393232 | tf_op jit(solution)/shard_map/psum | solution.py:257
  605.1 3.0 fusion.169
  610.3 14.7 %reduce-scatter.9.cloned.1.call-done = f32[128,384]{0,1:T(8,128)} async-done(((f32[512,384]{0,1:T(8,128)}), f32[128,384]{0,1:T(8,128)}) %reduce-scatter.9.cloned.1.call-update) | async-done | bytes 196624 | tf_op jit(solution)/shard_map/reduce_scatter | solution.py:151
  628.9 31.9 %all-reduce.28.cloned.1.call-done = f32[128,768]{1,0:T(8,128)} async-done(((f32[128,768]{1,0:T(8,128)}), f32[128,768]{1,0:T(8,128)}) %all-reduce.28.cloned.1.call-update) | async-done | bytes 393232 | tf_op jit(solution)/shard_map/psum | solution.py:278
  669.0 4.0 collective-permute-done.5
  676.4 3.0 fusion.160
  679.4 29.3 %all-reduce.30.cloned.1.call-done = f32[128,768]{1,0:T(8,128)} async-done(((f32[128,768]{1,0:T(8,128)}), f32[128,768]{1,0:T(8,128)}) %all-reduce.30.cloned.1.call-update) | async-done | bytes 393232 | tf_op jit(solution)/shard_map/psum | solution.py:257
  716.7 2.9 fusion.167
  719.7 4.8 add_bitcast_fusion.1
  729.8 10.0 reduce-scatter.11.cloned.1.call-done
  742.8 4.6 multiply_add_fusion
  750.3 26.4 %all-reduce.34.cloned.1.call-done = (f32[128,768]{1,0:T(8,128)}, f32[128,768]{1,0:T(8,128)}) async-done(((f32[128,768]{1,0:T(8,128)}, f32[128,768]{1,0:T(8,128)}), (f32[128,768]{1,0:T(8,128)}, f32[128,768]{1,0:T(8,128)})) %all-reduce.34.cloned.1.call-update) | async-done | bytes 786448 | tf_op jit(solution)/shard_map/psum | solution.py:199
  778.2 24.8 %all-reduce = (f32[1,2,768]{2,1,0:T(2,128)}, f32[1,2,768]{2,1,0:T(2,128)}, f32[1,2,192]{2,1,0:T(2,128)}, f32[1,768]{1,0:T(1,128)}, f32[1,768]{1,0:T(1,128)}, /*index=5*/f32[1,768]{1,0:T(1,128)}) all-reduce(f32[1,2,768]{2,1,0:T(2,128)S(1)} %fusion.232, ...), channel_id=1, replica_groups=mesh['section'=2,'tensor'=4,'dp'=4] {'dp'}, use_global_device_ids=true, to_apply=%region_96.97 | all-reduce | flops 5760 | bytes 46080 | tf_op jit(solution)/shard_map/psum | solution.py:373
  807.6 222.6 %all-reduce.32.cloned.1.call-done = (f32[1,768,3,192]{1,3,2,0:T(8,128)}, f32[1,192,768]{2,1,0:T(8,128)}, f32[1,768,768]{2,1,0:T(8,128)}, f32[1,768,768]{2,1,0:T(8,128)}) async-done(((f32[1,768,3,192]{1,3,2,0:T(8,128)}, f32[1,192,768]{2,1,0:T(8,128)}, f32[1,768,768]{2,1,0:T(8,128)}, f32[1,768,768]{2,1,0:T(8,128)}), (f32[1,768,3,192]{1,3,2,0:T(8,128)}, f32[1,192,768]{2,1,0:T(8,128)}, ...) | async-done | bytes 7077904 | tf_op jit(solution)/shard_map/psum | solution.py:373
  1030.2 2.9 copy.45
  (816 shorter events, 195.6 us)
Async XLA Ops:
  7.2 73.0 %copy-start = (bf16[1,768,768]{2,1,0:T(8,128)(2,1)S(1)}, bf16[1,768,768]{2,1,0:T(8,128)(2,1)}, u32[]{:S(2)}) copy-start(bf16[1,768,768]{2,1,0:T(8,128)(2,1)} %param.23) | copy-start | bytes 3538948
  7.2 70.4 %all-reduce.20.cloned.1.call-start = ((), (), s32[]{:S(2)}) async-start(), calls=%async_computation.4 | async-start | bytes 786432 | tf_op jit(solution)/shard_map/psum | solution.py:191
  45.8 68.3 %all-reduce.22.cloned.1.call-start = ((), (), s32[]{:S(2)}) async-start(), calls=%async_computation.5 | async-start | bytes 786432 | tf_op jit(solution)/shard_map/psum | solution.py:199
  52.2 61.9 %copy-start.137 = (f32[768]{0:T(1024)}, f32[768]{0:T(1024)S(1)}, u32[]{:S(2)}) copy-start(f32[768]{0:T(1024)S(1)} %reduce.16) | copy-start | bytes 9220
  81.3 131.5 %all-reduce.24.cloned.1.call-start = ((), (), s32[]{:S(2)}) async-start(), calls=%async_computation.6 | async-start | bytes 786432 | tf_op jit(solution)/shard_map/psum | solution.py:191
  115.3 6.7 collective-permute-start
  123.0 55.3 %copy-start.109 = (pred[128,512]{1,0:T(8,128)(4,1)S(1)}, pred[128,512]{1,0:T(8,128)(4,1)}, u32[]{:S(2)}) copy-start(pred[128,512]{1,0:T(8,128)(4,1)} %broadcast_compare_fusion.6) | copy-start | bytes 196612
  123.5 55.2 %copy-start.233 = (f32[128]{0:T(128)}, f32[128]{0:T(128)S(1)}, u32[]{:S(2)}) copy-start(f32[128]{0:T(128)S(1)} %add_rsqrt_fusion.5) | copy-start | bytes 1540
  124.0 55.0 %copy-start.165 = (f32[3,128]{1,0:T(4,128)S(1)}, f32[3,128]{1,0:T(4,128)}, u32[]{:S(2)}) copy-start(f32[3,128]{1,0:T(4,128)} %copy-done.164) | copy-start | bytes 4612
  125.7 52.6 %copy-start.123 = (bf16[128,192]{0,1:T(8,128)(2,1)}, bf16[128,192]{0,1:T(8,128)(2,1)S(1)}, u32[]{:S(2)}) copy-start(bf16[128,192]{0,1:T(8,128)(2,1)S(1)} %get-tuple-element.138) | copy-start | bytes 147460
  125.7 54.3 %copy-start.113 = (bf16[128,192]{0,1:T(8,128)(2,1)}, bf16[128,192]{0,1:T(8,128)(2,1)S(1)}, u32[]{:S(2)}) copy-start(bf16[128,192]{0,1:T(8,128)(2,1)S(1)} %get-tuple-element.166) | copy-start | bytes 147460
  125.7 54.3 %copy-start.121 = (bf16[128,192]{0,1:T(8,128)(2,1)}, bf16[128,192]{0,1:T(8,128)(2,1)S(1)}, u32[]{:S(2)}) copy-start(bf16[128,192]{0,1:T(8,128)(2,1)S(1)} %get-tuple-element.168) | copy-start | bytes 147460
  181.0 76.6 %all-reduce.42.cloned.1.call-start = ((), (), s32[]{:S(2)}) async-start(), calls=%async_computation.19 | async-start | bytes 1572864 | tf_op jit(solution)/shard_map/psum | solution.py:199
  222.7 89.9 %reduce-scatter.5.cloned.1.call-start = ((), (), s32[]{:S(2)}) async-start(), calls=%async_computation.7 | async-start | bytes 983040 | tf_op jit(solution)/shard_map/reduce_scatter | solution.py:151
  263.8 9.9 collective-permute-start.1
  270.9 76.6 %all-reduce.40.cloned.1.call-start = ((), (), s32[]{:S(2)}) async-start(), calls=%async_computation.18 | async-start | bytes 1572864 | tf_op jit(solution)/shard_map/psum | solution.py:191
  315.9 85.7 %all-reduce.38.cloned.1.call-start = ((), (), s32[]{:S(2)}) async-start(), calls=%async_computation.17 | async-start | bytes 1572864 | tf_op jit(solution)/shard_map/psum | solution.py:199
  352.2 8.2 collective-permute-start.3
  364.8 133.7 %reduce-scatter.7.cloned.1.call-start = ((), (), s32[]{:S(2)}) async-start(), calls=%async_computation.8 | async-start | bytes 983040 | tf_op jit(solution)/shard_map/reduce_scatter | solution.py:151
  367.9 35.7 %copy-start.221 = (f32[128]{0:T(128)S(1)}, f32[128]{0:T(128)}, u32[]{:S(2)}) copy-start(f32[128]{0:T(128)} %broadcast_multiply_fusion.5) | copy-start | bytes 1540
  408.0 9.8 collective-permute-start.2
  415.0 118.9 %all-reduce.36.cloned.1.call-start = ((), (), s32[]{:S(2)}) async-start(), calls=%async_computation.16 | async-start | bytes 1572864 | tf_op jit(solution)/shard_map/psum | solution.py:191
  421.8 58.3 %copy-start.50 = (f32[128,768]{1,0:T(8,128)}, f32[128,768]{1,0:T(8,128)S(1)}, u32[]{:S(2)}) copy-start(f32[128,768]{1,0:T(8,128)S(1)} %get-tuple-element.151) | copy-start | bytes 1179652
  421.9 57.9 %copy-start.107 = (pred[128,512]{1,0:T(8,128)(4,1)S(1)}, pred[128,512]{1,0:T(8,128)(4,1)}, u32[]{:S(2)}) copy-start(pred[128,512]{1,0:T(8,128)(4,1)} %broadcast_compare_fusion.4) | copy-start | bytes 196612
  440.0 54.6 %copy-start.204 = (f32[3,128]{1,0:T(4,128)S(1)}, f32[3,128]{1,0:T(4,128)}, u32[]{:S(2)}) copy-start(f32[3,128]{1,0:T(4,128)} %copy-done.203) | copy-start | bytes 4612
  440.0 55.2 %copy-start.202 = (f32[3,128]{1,0:T(4,128)S(1)}, f32[3,128]{1,0:T(4,128)}, u32[]{:S(2)}) copy-start(f32[3,128]{1,0:T(4,128)} %copy-done.201) | copy-start | bytes 4612
  440.0 55.8 %copy-start.114 = (bf16[128,192]{0,1:T(8,128)(2,1)S(1)}, bf16[128,192]{0,1:T(8,128)(2,1)}, u32[]{:S(2)}) copy-start(bf16[128,192]{0,1:T(8,128)(2,1)} %copy-done.113) | copy-start | bytes 147460
  440.0 56.4 %copy-start.150 = (bf16[3,64,128]{2,1,0:T(8,128)(2,1)S(1)}, bf16[3,64,128]{2,1,0:T(8,128)(2,1)}, u32[]{:S(2)}) copy-start(bf16[3,64,128]{2,1,0:T(8,128)(2,1)} %copy-done.149) | copy-start | bytes 147460
  440.0 56.4 %copy-start.152 = (bf16[3,64,128]{2,1,0:T(8,128)(2,1)S(1)}, bf16[3,64,128]{2,1,0:T(8,128)(2,1)}, u32[]{:S(2)}) copy-start(bf16[3,64,128]{2,1,0:T(8,128)(2,1)} %copy-done.151) | copy-start | bytes 147460
  440.0 56.4 %copy-start.154 = (bf16[3,64,128]{2,1,0:T(8,128)(2,1)S(1)}, bf16[3,64,128]{2,1,0:T(8,128)(2,1)}, u32[]{:S(2)}) copy-start(bf16[3,64,128]{2,1,0:T(8,128)(2,1)} %copy-done.153) | copy-start | bytes 147460
  452.9 40.8 %copy-start.219 = (f32[128]{0:T(128)}, f32[128]{0:T(128)S(1)}, u32[]{:S(2)}) copy-start(f32[128]{0:T(128)S(1)} %broadcast_multiply_fusion.4) | copy-start | bytes 1540
  499.4 105.7 %copy-start.83 = (bf16[128,384]{0,1:T(8,128)(2,1)}, bf16[128,384]{0,1:T(8,128)(2,1)S(1)}, u32[]{:S(2)}) copy-start(bf16[128,384]{0,1:T(8,128)(2,1)S(1)} %convert.37) | copy-start | bytes 294916
  501.8 90.5 %all-reduce.26.cloned.1.call-start = ((), (), s32[]{:S(2)}) async-start(), calls=%async_computation.9 | async-start | bytes 786432 | tf_op jit(solution)/shard_map/psum | solution.py:257
  547.7 7.7 collective-permute-start.4
  559.7 65.3 %reduce-scatter.9.cloned.1.call-start = ((), (), s32[]{:S(2)}) async-start(), calls=%async_computation.10 | async-start | bytes 983040 | tf_op jit(solution)/shard_map/reduce_scatter | solution.py:151
  601.5 59.4 %all-reduce.28.cloned.1.call-start = ((), (), s32[]{:S(2)}) async-start(), calls=%async_computation.11 | async-start | bytes 786432 | tf_op jit(solution)/shard_map/psum | solution.py:278
  609.4 51.5 %copy-start.217 = (f32[128]{0:T(128)S(1)}, f32[128]{0:T(128)}, u32[]{:S(2)}) copy-start(f32[128]{0:T(128)} %broadcast_multiply_fusion.2) | copy-start | bytes 1540
  609.4 51.5 %copy-start.239 = (f32[128]{0:T(128)S(1)}, f32[128]{0:T(128)}, u32[]{:S(2)}) copy-start(f32[128]{0:T(128)} %fusion.253) | copy-start | bytes 1540
  609.4 53.5 %copy-start.242 = (f32[128]{0:T(128)S(1)}, f32[128]{0:T(128)}, u32[]{:S(2)}) copy-start(f32[128]{0:T(128)} %multiply_reduce_fusion.17) | copy-start | bytes 1540
  610.3 54.1 %copy-start.115 = (bf16[3,64,128]{2,1,0:T(8,128)(2,1)}, bf16[3,64,128]{2,1,0:T(8,128)(2,1)S(1)}, u32[]{:S(2)}) copy-start(bf16[3,64,128]{2,1,0:T(8,128)(2,1)S(1)} %get-tuple-element.208) | copy-start | bytes 147460
  628.9 79.8 %all-reduce.30.cloned.1.call-start = ((), (), s32[]{:S(2)}) async-start(), calls=%async_computation.12 | async-start | bytes 786432 | tf_op jit(solution)/shard_map/psum | solution.py:257
  665.4 7.7 collective-permute-start.5
  676.4 63.4 %reduce-scatter.11.cloned.1.call-start = ((), (), s32[]{:S(2)}) async-start(), calls=%async_computation.13 | async-start | bytes 983040 | tf_op jit(solution)/shard_map/reduce_scatter | solution.py:151
  716.3 60.4 %all-reduce.34.cloned.1.call-start = ((), (), s32[]{:S(2)}) async-start(), calls=%async_computation.15 | async-start | bytes 1572864 | tf_op jit(solution)/shard_map/psum | solution.py:199
  742.7 287.6 %all-reduce.32.cloned.1.call-start = ((), (), s32[]{:S(2)}) async-start(), calls=%async_computation.14 | async-start | bytes 14155776 | tf_op jit(solution)/shard_map/psum | solution.py:373
  747.7 55.3 %copy-start.12 = (f32[128,768]{1,0:T(8,128)S(1)}, f32[128,768]{1,0:T(8,128)}, u32[]{:S(2)}) copy-start(f32[128,768]{1,0:T(8,128)} %get-tuple-element.103) | copy-start | bytes 1179652
  747.7 55.3 %copy-start.140 = (f32[768]{0:T(1024)S(1)}, f32[768]{0:T(1024)}, u32[]{:S(2)}) copy-start(f32[768]{0:T(1024)} %copy-done.137) | copy-start | bytes 9220
  747.7 56.5 %copy-start.90 = (bf16[1,128,768]{2,1,0:T(8,128)(2,1)S(1)}, bf16[1,128,768]{2,1,0:T(8,128)(2,1)}, u32[]{:S(2)}) copy-start(bf16[1,128,768]{2,1,0:T(8,128)(2,1)} %get-tuple-element.87) | copy-start | bytes 589828
  (222 other events, 1783.7 us)
Sparse Core Ops, SparseCore 0:
  45.9 31.6 all-reduce.19
  81.4 32.5 all-reduce.21
  181.2 31.6 all-reduce.23
  222.8 34.7 all-reduce.41
  271.0 25.3 reduce-scatter.4
  316.0 31.4 all-reduce.39
  364.9 36.6 all-reduce.37
  415.2 25.2 reduce-scatter.6
  501.9 32.0 all-reduce.35
  559.8 32.4 all-reduce.25
  601.6 23.3 reduce-scatter.8
  629.0 31.8 all-reduce.27
  676.5 32.1 all-reduce.29
  716.5 23.2 reduce-scatter.10
  742.8 33.9 all-reduce.33
  780.4 249.7 all-reduce.31
where the time goes:
time: 1060 us; the launch traced here: 1040 us
  waiting for transfers between devices  541 us (51%)
  blocking collectives  241 us (23%)
  other arithmetic  111 us (10%)
  matrix products  96.6 us (9%)
  local copies, waits for them, and re-layouts  20.8 us (2%)
  between operations  19 us (2%)
  starting transfers between devices  16.7 us (2%)
    psum x1, waiting for transfers between devices, per_device(): summed = lax.psum(totals, 'dp')  223 us
    psum x4, waiting for transfers between devices, layer_forward(): lax.psum(jnp.dot(active, proj_weight, preferred_element_type=jnp.float32)...  121 us
    psum x4, waiting for transfers between devices, layer_forward(): lax.psum(jnp.dot(attended, out_weight, preferred_element_type=jnp.float32...  68.8 us
    psum x2, waiting for transfers between devices, layer_backward(): grad_normed_mid = lax.psum(contract_cols(grad_pre, fc_weight), 'tensor')  60.6 us
    all_gather x4, blocking collectives, attend_forward(): lax.all_gather(keys, 'dp', axis=0, tiled=True)  58.4 us
    all_gather x4, blocking collectives, attend_backward(): lax.all_gather(keys, 'dp', axis=0, tiled=True)  53.4 us
    all_gather x4, blocking collectives, attend_backward(): lax.all_gather(values, 'dp', axis=0, tiled=True)  53.1 us
    all_gather x4, blocking collectives, attend_forward(): lax.all_gather(values, 'dp', axis=0, tiled=True)  50.9 us
  transfers between devices with their start and end apart: 22, of which 17 were waited for; matrix products, arithmetic and copies ran while one was open for 10% of the time, Pallas kernels for 0%

commit v1 on v0

v1 whole, which is shorter than its diff:
```python
import functools
import math

import jax
import jax.numpy as jnp
from jax import lax
from jax.experimental import pallas as pl
from jax.experimental.pallas import tpu as pltpu
from jax.sharding import PartitionSpec as P

HEAD = 64


EPSILON = 1e-05
MASKED = -1e30
GELU_RATE = 0.7978845608028654
GELU_CUBE = 0.044715
MESH = pl.DeviceIdType.MESH
VMEM_BYTES = 48 * 1024 * 1024


def passed_along(block, axis, distance):
    devices = range(lax.axis_size(axis))
    route = [(i - distance, i) for i in devices if i - distance in devices]
    return lax.ppermute(block, axis, route)


def layer_norm(values, gains, biases):
    average = jnp.mean(values, axis=-1, keepdims=True)
    centered = values - average
    spread = jnp.mean(centered * centered, axis=-1, keepdims=True)
    return centered * lax.rsqrt(spread + EPSILON) * gains + biases


def gelu_tanh(values):
    return (
        0.5 * values * (1.0 + jnp.tanh(GELU_RATE * (values + GELU_CUBE * values * values * values)))
    )


def contract_rows(left, right):
    return lax.dot_general(
        left, right, (((0,), (0,)), ((), ())), preferred_element_type=jnp.float32
    )


def contract_cols(left, right):
    return lax.dot_general(
        left, right, (((1,), (1,)), ((), ())), preferred_element_type=jnp.float32
    )


def meet(axis, partners):
    barrier = pltpu.get_barrier_semaphore()
    for partner in partners:
        pl.semaphore_signal(barrier, inc=1, device_id={axis: partner}, device_id_type=MESH)
    pl.semaphore_wait(barrier, len(partners))


def meet_line(axis, me, count):
    barrier = pltpu.get_barrier_semaphore()

    @pl.when(me > 0)
    def _():
        pl.semaphore_signal(barrier, inc=1, device_id={axis: me - 1}, device_id_type=MESH)

    @pl.when(me < count - 1)
    def _():
        pl.semaphore_signal(barrier, inc=1, device_id={axis: me + 1}, device_id_type=MESH)

    neighbours = (me > 0).astype(jnp.int32) + (me < count - 1).astype(jnp.int32)
    pl.semaphore_wait(barrier, neighbours)


def sum_tensor_kernel(pieces, x_ref, o_ref, away, first, mine, second, last, send, recv):
    me = lax.axis_index("tensor")
    parity = lax.rem(me, 2)
    near = me + 1 - 2 * parity
    far = lax.rem(me + 2, 4)
    half = x_ref.shape[0] // 2
    rows = half // pieces
    meet("tensor", (near, far))

    def copy(source, target, step, k, device):
        span = pl.ds(k * rows, rows)
        return pltpu.make_async_remote_copy(
            src_ref=source.at[span],
            dst_ref=target.at[span],
            send_sem=send.at[step, k],
            recv_sem=recv.at[step, k],
            device_id={"tensor": device},
            device_id_type=MESH,
        )

    copies = [[None] * pieces for _ in range(3)]
    for k in range(pieces):
        span = pl.ds(k * rows, rows)
        begin = pl.multiple_of((1 - parity) * half + k * rows, 16)
        away[span] = x_ref[pl.ds(begin, rows)].astype(jnp.bfloat16)
        copies[0][k] = copy(away, first, 0, k, near)
        copies[0][k].start()
    for k in range(pieces):
        span = pl.ds(k * rows, rows)
        begin = pl.multiple_of(parity * half + k * rows, 16)
        copies[0][k].wait_recv()
        mine[span] = (x_ref[pl.ds(begin, rows)] + first[span].astype(jnp.float32)).astype(
            jnp.bfloat16
        )
        copies[1][k] = copy(mine, second, 1, k, far)
        copies[1][k].start()
    for k in range(pieces):
        span = pl.ds(k * rows, rows)
        begin = pl.multiple_of(parity * half + k * rows, 16)
        copies[1][k].wait_recv()
        copies[0][k].wait_send()
        away[span] = (mine[span].astype(jnp.float32) + second[span].astype(jnp.float32)).astype(
            jnp.bfloat16
        )
        copies[2][k] = copy(away, last, 2, k, near)
        copies[2][k].start()
        o_ref[pl.ds(begin, rows)] = away[span].astype(jnp.float32)
    for k in range(pieces):
        span = pl.ds(k * rows, rows)
        begin = pl.multiple_of((1 - parity) * half + k * rows, 16)
        copies[2][k].wait_recv()
        o_ref[pl.ds(begin, rows)] = last[span].astype(jnp.float32)
    for k in range(pieces):
        copies[1][k].wait_send()
        copies[2][k].wait_send()


def sum_tensor(partial):
    rows, width = partial.shape
    if lax.axis_size("tensor") != 4 or rows % 96:
        return lax.psum(partial, "tensor")
    half = pltpu.VMEM((rows // 2, width), jnp.bfloat16)
    pieces = 3
    return pl.pallas_call(
        functools.partial(sum_tensor_kernel, pieces),
        out_shape=jax.ShapeDtypeStruct((rows, width), jnp.float32),
        in_specs=[pl.BlockSpec(memory_space=pltpu.VMEM)],
        out_specs=pl.BlockSpec(memory_space=pltpu.VMEM),
        scratch_shapes=[half] * 5
        + [pltpu.SemaphoreType.DMA((3, pieces)), pltpu.SemaphoreType.DMA((3, pieces))],
        compiler_params=pltpu.CompilerParams(
            collective_id=0, has_side_effects=True, vmem_limit_bytes=VMEM_BYTES
        ),
    )(partial)


def gather_kernel(count, x_ref, o_ref, send, recv):
    me = lax.axis_index("dp")
    batches = x_ref.shape[0]
    meet_line("dp", me, count)
    o_ref[me] = x_ref[...]

    def copy(side, step, m):
        owner = me - step if side == 0 else me + step
        return pltpu.make_async_remote_copy(
            src_ref=o_ref.at[owner, m],
            dst_ref=o_ref.at[owner, m],
            send_sem=send.at[side, step, m],
            recv_sem=recv.at[side, step, m],
            device_id={"dp": me + 1 if side == 0 else me - 1},
            device_id_type=MESH,
        )

    def arrival(side, step, m):
        owner = me - 1 - step if side == 0 else me + 1 + step
        return pltpu.make_async_remote_copy(
            src_ref=o_ref.at[owner, m],
            dst_ref=o_ref.at[owner, m],
            send_sem=send.at[side, step, m],
            recv_sem=recv.at[side, step, m],
            device_id={"dp": me - 1 if side == 0 else me + 1},
            device_id_type=MESH,
        )

    def sends(side, step):
        if side == 0:
            return jnp.logical_and(me < count - 1, me - step >= 0)
        return jnp.logical_and(me > 0, me + step <= count - 1)

    def arrives(side, step):
        return me - 1 - step >= 0 if side == 0 else me + 1 + step <= count - 1

    for step in range(count - 1):
        for m in range(batches):
            for side in range(2):
                if step:

                    @pl.when(arrives(side, step - 1))
                    def _():
                        arrival(side, step - 1, m).wait_recv()

                @pl.when(sends(side, step))
                def _():
                    copy(side, step, m).start()

    for m in range(batches):
        for side in range(2):

            @pl.when(arrives(side, count - 2))
            def _():
                arrival(side, count - 2, m).wait_recv()

    for step in range(count - 1):
        for m in range(batches):
            for side in range(2):

                @pl.when(sends(side, step))
                def _():
                    copy(side, step, m).wait_send()


def gather_dp(block):
    count = lax.axis_size("dp")
    batches = block.shape[0]
    if count == 1:
        return block[None]
    semaphores = pltpu.SemaphoreType.DMA((2, count - 1, batches))
    return pl.pallas_call(
        functools.partial(gather_kernel, count),
        out_shape=jax.ShapeDtypeStruct((count,) + block.shape, block.dtype),
        in_specs=[pl.BlockSpec(memory_space=pltpu.VMEM)],
        out_specs=pl.BlockSpec(memory_space=pltpu.VMEM),
        scratch_shapes=[semaphores, semaphores],
        compiler_params=pltpu.CompilerParams(
            collective_id=1, has_side_effects=True, vmem_limit_bytes=VMEM_BYTES
        ),
    )(block)


def scatter_kernel(count, x_ref, o_ref, landed, send, recv):
    me = lax.axis_index("dp")
    batches = x_ref.shape[1]
    meet_line("dp", me, count)

    def copy(side, step, m, source):
        return pltpu.make_async_remote_copy(
            src_ref=source,
            dst_ref=landed.at[side, step, m],
            send_sem=send.at[side, step, m],
            recv_sem=recv.at[side, step, m],
            device_id={"dp": me + 1 if side == 0 else me - 1},
            device_id_type=MESH,
        )

    for step in range(count - 1):
        for m in range(batches):
            for side in range(2):
                owner = count - 1 - step if side == 0 else step
                at_end = me == 0 if side == 0 else me == count - 1
                inside = (
                    jnp.logical_and(me > 0, me < owner)
                    if side == 0
                    else jnp.logical_and(me < count - 1, me > owner)
                )

                @pl.when(at_end)
                def _():
                    copy(side, step, m, x_ref.at[owner, m]).start()

                @pl.when(inside)
                def _():
                    copy(side, step, m, landed.at[side, step, m]).wait_recv()
                    landed[side, step, m] = (
                        landed[side, step, m].astype(jnp.float32)
                        + x_ref[owner, m].astype(jnp.float32)
                    ).astype(jnp.bfloat16)
                    copy(side, step, m, landed.at[side, step, m]).start()

    for m in range(batches):
        o_ref[m] = x_ref[me, m].astype(jnp.float32)
        for side in range(2):
            step = count - 1 - me if side == 0 else me

            @pl.when(me > 0 if side == 0 else me < count - 1)
            def _():
                copy(side, step, m, landed.at[side, step, m]).wait_recv()
                o_ref[m] += landed[side, step, m].astype(jnp.float32)

    for step in range(count - 1):
        for m in range(batches):
            for side in range(2):
                owner = count - 1 - step if side == 0 else step

                @pl.when(me < owner if side == 0 else me > owner)
                def _():
                    copy(side, step, m, x_ref.at[owner, m]).wait_send()


def scatter_dp(terms):
    count, batches, rows, width = terms.shape
    if count == 1:
        return terms[0].astype(jnp.float32)
    semaphores = pltpu.SemaphoreType.DMA((2, count - 1, batches))
    return pl.pallas_call(
        functools.partial(scatter_kernel, count),
        out_shape=jax.ShapeDtypeStruct((batches, rows, width), jnp.float32),
        in_specs=[pl.BlockSpec(memory_space=pltpu.VMEM)],
        out_specs=pl.BlockSpec(memory_space=pltpu.VMEM),
        scratch_shapes=[
            pltpu.VMEM((2, count - 1, batches, rows, width), jnp.bfloat16),
            semaphores,
            semaphores,
        ],
        compiler_params=pltpu.CompilerParams(
            collective_id=2, has_side_effects=True, vmem_limit_bytes=VMEM_BYTES
        ),
    )(terms.astype(jnp.bfloat16))


def layer_forward(inputs, allowed, params):
    (
        gains,
        biases,
        qkv_weight,
        qv_bias,
        out_weight,
        out_bias,
        fc_weight,
        fc_bias,
        proj_weight,
        proj_bias,
    ) = params
    batches, _, shard_rows, key_count = allowed.shape
    local_width = qkv_weight.shape[2]
    head_count = local_width // HEAD
    normed = layer_norm(inputs, gains[0], biases[0]).astype(jnp.bfloat16)
    projected = jnp.dot(
        normed,
        qkv_weight.reshape(qkv_weight.shape[0], 3 * local_width),
        preferred_element_type=jnp.float32,
    )
    query = (projected[:, :local_width] + qv_bias[0]).astype(jnp.bfloat16)
    keys = projected[:, local_width : 2 * local_width].astype(jnp.bfloat16)
    values = (projected[:, 2 * local_width :] + qv_bias[1]).astype(jnp.bfloat16)
    pair = jnp.concatenate([keys, values], axis=1).reshape(batches, shard_rows, 2 * local_width)
    gathered = gather_dp(pair)
    gathered = gathered.transpose(1, 0, 2, 3).reshape(batches, key_count, 2, head_count, HEAD)
    key_heads = gathered[:, :, 0]
    value_heads = gathered[:, :, 1]
    queries = query.reshape(batches, shard_rows, head_count, HEAD)
    scores = jnp.einsum(
        "mqhe,mkhe->mhqk", queries, key_heads, preferred_element_type=jnp.float32
    ) * (1.0 / math.sqrt(HEAD))
    scores = jnp.where(allowed, scores, MASKED)
    peak = jnp.max(scores, axis=-1, keepdims=True)
    powers = jnp.where(allowed, jnp.exp(scores - peak), 0.0)
    softmax = powers / jnp.sum(powers, axis=-1, keepdims=True)
    attended = jnp.einsum(
        "mhqk,mkhe->mqhe",
        softmax.astype(jnp.bfloat16),
        value_heads,
        preferred_element_type=jnp.float32,
    )
    attended = attended.reshape(batches * shard_rows, local_width).astype(jnp.bfloat16)
    middle = (
        inputs
        + sum_tensor(jnp.dot(attended, out_weight, preferred_element_type=jnp.float32))
        + out_bias
    )
    normed_mid = layer_norm(middle, gains[1], biases[1]).astype(jnp.bfloat16)
    hidden_pre = jnp.dot(normed_mid, fc_weight, preferred_element_type=jnp.float32) + fc_bias
    active = gelu_tanh(hidden_pre).astype(jnp.bfloat16)
    output = (
        middle
        + sum_tensor(jnp.dot(active, proj_weight, preferred_element_type=jnp.float32))
        + proj_bias
    )
    saved_state = (
        inputs,
        normed,
        queries,
        key_heads,
        value_heads,
        softmax,
        attended,
        middle,
        normed_mid,
        hidden_pre,
        active,
    )
    return (output, saved_state)


def layer_backward(grad_output, saved_state, params, with_grads):
    (
        gains,
        biases,
        qkv_weight,
        qv_bias,
        out_weight,
        out_bias,
        fc_weight,
        fc_bias,
        proj_weight,
        proj_bias,
    ) = params
    (
        inputs,
        normed,
        queries,
        key_heads,
        value_heads,
        softmax,
        attended,
        middle,
        normed_mid,
        hidden_pre,
        active,
    ) = saved_state
    batches, shard_rows, head_count, _ = queries.shape
    rows = batches * shard_rows
    local_width = head_count * HEAD
    key_count = key_heads.shape[1]
    score_scale = 1.0 / math.sqrt(HEAD)

    def summed(member):
        return lax.psum(member.astype(jnp.bfloat16), "dp").astype(jnp.float32)

    grad_low = grad_output.astype(jnp.bfloat16)
    grad_active = contract_cols(grad_low, proj_weight)
    grad_pre = jax.vjp(gelu_tanh, hidden_pre)[1](grad_active)[0].astype(jnp.bfloat16)
    grad_normed_mid = sum_tensor(contract_cols(grad_pre, fc_weight))
    if with_grads:
        grad_proj_weight = summed(contract_rows(active, grad_low))
        grad_fc_weight = summed(contract_rows(normed_mid, grad_pre))
    grad_middle_norm, grad_gain_mid, grad_bias_mid = jax.vjp(
        layer_norm, middle, gains[1], biases[1]
    )[1](grad_normed_mid)
    grad_middle = grad_output + grad_middle_norm
    middle_low = grad_middle.astype(jnp.bfloat16)
    grad_attended = contract_cols(middle_low, out_weight).astype(jnp.bfloat16)
    if with_grads:
        grad_out_weight = summed(contract_rows(attended, middle_low))
    grad_heads = grad_attended.reshape(batches, shard_rows, head_count, HEAD)
    grad_softmax = jnp.einsum(
        "mqhe,mkhe->mhqk", grad_heads, value_heads, preferred_element_type=jnp.float32
    )
    delta = jnp.sum(softmax * grad_softmax, axis=-1, keepdims=True)
    grad_scores = (softmax * (grad_softmax - delta)).astype(jnp.bfloat16)
    grad_query = (
        jnp.einsum("mhqk,mkhe->mqhe", grad_scores, key_heads, preferred_element_type=jnp.float32)
        * score_scale
    )
    grad_keys = (
        jnp.einsum("mhqk,mqhe->mkhe", grad_scores, queries, preferred_element_type=jnp.float32)
        * score_scale
    )
    grad_values = jnp.einsum(
        "mhqk,mqhe->mkhe",
        softmax.astype(jnp.bfloat16),
        grad_heads,
        preferred_element_type=jnp.float32,
    )
    terms = jnp.concatenate(
        [
            grad_keys.reshape(batches, key_count, local_width),
            grad_values.reshape(batches, key_count, local_width),
        ],
        axis=2,
    ).astype(jnp.bfloat16)
    terms = terms.reshape(batches, key_count // shard_rows, shard_rows, 2 * local_width)
    key_grads = scatter_dp(terms.transpose(1, 0, 2, 3)).reshape(rows, 2 * local_width)
    grad_query = grad_query.reshape(rows, local_width).astype(jnp.bfloat16)
    grad_keys = key_grads[:, :local_width].astype(jnp.bfloat16)
    grad_values = key_grads[:, local_width:].astype(jnp.bfloat16)
    grad_projected = jnp.concatenate([grad_query, grad_keys, grad_values], axis=1)
    qkv_flat = qkv_weight.reshape(qkv_weight.shape[0], -1)
    if with_grads:
        grad_qkv_weight = summed(contract_rows(normed, grad_projected)).reshape(qkv_weight.shape)
    grad_normed = sum_tensor(contract_cols(grad_projected, qkv_flat))
    grad_input_norm, grad_gain_in, grad_bias_in = jax.vjp(layer_norm, inputs, gains[0], biases[0])[
        1
    ](grad_normed)
    grad_input = grad_middle + grad_input_norm
    if not with_grads:
        return (grad_input, None)
    small = jnp.concatenate(
        [
            grad_gain_in,
            grad_gain_mid,
            grad_bias_in,
            grad_bias_mid,
            jnp.sum(grad_query.astype(jnp.float32), axis=0),
            jnp.sum(grad_values.astype(jnp.float32), axis=0),
            jnp.sum(grad_middle, axis=0),
            jnp.sum(grad_pre.astype(jnp.float32), axis=0),
            jnp.sum(grad_output, axis=0),
        ]
    )
    small = lax.psum(small, "dp")
    width = gains.shape[1]
    sizes = (2 * width, 2 * width, 2 * local_width, width, fc_bias.shape[0], width)
    parts = []
    begin = 0
    for size in sizes:
        parts.append(small[begin : begin + size])
        begin += size
    grads = (
        parts[0].reshape(gains.shape),
        parts[1].reshape(biases.shape),
        grad_qkv_weight,
        parts[2].reshape(qv_bias.shape),
        grad_out_weight,
        parts[3],
        grad_fc_weight,
        parts[4],
        grad_proj_weight,
        parts[5],
    )
    return (grad_input, grads)


def per_device(
    tokens,
    block_order,
    ln_gain,
    ln_bias,
    qkv_weight,
    qv_bias,
    out_weight,
    out_bias,
    fc_weight,
    fc_bias,
    proj_weight,
    proj_bias,
    cotangent,
):
    micro_count, shard_rows, model_width = tokens.shape
    is_first = lax.axis_index("section") == 0
    dp_index = lax.axis_index("dp")
    params = (
        ln_gain[0],
        ln_bias[0],
        qkv_weight[0],
        qv_bias[0],
        out_weight[0],
        out_bias[0],
        fc_weight[0],
        fc_bias[0],
        proj_weight[0],
        proj_bias[0],
    )
    row_offsets = jnp.arange(shard_rows, dtype=jnp.int32)
    positions = block_order[:, :, None] * shard_rows + row_offsets
    key_pos = positions.reshape(micro_count, -1)
    query_pos = block_order[:, dp_index][:, None] * shard_rows + row_offsets
    allowed = (query_pos[:, :, None] >= key_pos[:, None, :])[:, None]
    rows = micro_count * shard_rows
    inputs = tokens.reshape(rows, model_width).astype(jnp.float32)
    output, _ = layer_forward(inputs, allowed, params)
    received = passed_along(output.astype(jnp.bfloat16), "section", 1).astype(jnp.float32)
    inputs = jnp.where(is_first, inputs, received)
    output, saved_state = layer_forward(inputs, allowed, params)
    seed_grad = cotangent.reshape(rows, model_width).astype(jnp.float32)
    grad_input, _ = layer_backward(seed_grad, saved_state, params, False)
    received = passed_along(grad_input.astype(jnp.bfloat16), "section", -1).astype(jnp.float32)
    grad_output = jnp.where(is_first, received, seed_grad)
    grad_input, grads = layer_backward(grad_output, saved_state, params, True)
    section_out = output.astype(jnp.bfloat16).reshape(tokens.shape)[None]
    section_grad = grad_input.reshape(tokens.shape)[None]
    return (section_out, section_grad) + tuple((member[None] for member in grads))


def solution(mesh):
    return jax.shard_map(
        per_device,
        mesh=mesh,
        in_specs=(
            P(None, "dp", None),
            P(),
            P("section", None, None),
            P("section", None, None),
            P("section", None, None, "tensor"),
            P("section", None, "tensor"),
            P("section", "tensor", None),
            P("section", None),
            P("section", None, "tensor"),
            P("section", "tensor"),
            P("section", "tensor", None),
            P("section", None),
            P(None, "dp", None),
        ),
        out_specs=(
            P("section", None, "dp", None),
            P("section", None, "dp", None),
            P("section", None, None),
            P("section", None, None),
            P("section", None, None, "tensor"),
            P("section", None, "tensor"),
            P("section", "tensor", None),
            P("section", None),
            P("section", None, "tensor"),
            P("section", "tensor"),
            P("section", "tensor", None),
            P("section", None),
        ),
        check_vma=False,
    )
```

time: 1060 us -> 481 us (0.45)
  waiting for transfers between devices: 541 us -> 101 us
  blocking collectives: 241 us -> 20.4 us
  Pallas kernels: 0 us -> 201 us
  other arithmetic: 111 us -> 34.5 us
  matrix products: 96.6 us -> 48.1 us
  local copies, waits for them, and re-layouts: 20.8 us -> 47.7 us
  starting transfers between devices: 16.7 us -> 4.76 us
    psum x12 -> x1, waiting for transfers between devices: 505 us -> 83.8 us  [summed(): return lax.psum(member.astype(jnp.bfloat16), 'dp').astype(jnp.float32)]
    all_gather x16 -> x0, blocking collectives: 216 us -> none  [the longest x4 58.4 us: attend_forward(): lax.all_gather(keys, 'dp', axis=0, tiled=True)]
    pallas_call x0 -> x12, Pallas kernels: none -> 201 us  [the longest x8 91.9 us: sum_tensor(): pl.pallas_call(functools.partial(sum_tensor_kernel, pieces), out_shape=ja...]
    dot_general x16 -> x4, matrix products: 42.6 us -> 6.98 us  [contract_rows(): lax.dot_general(left, right, (((0,), (0,)), ((), ())), preferred_element_...]
    reduce_scatter x4 -> x0, waiting for transfers between devices: 24.6 us -> none  [attend_backward(): lax.psum_scatter(key_terms, 'dp', scatter_dimension=0, tiled=True)]
    concatenate x0 -> x11, local copies, waits for them, and re-layouts: none -> 15.9 us  [the longest x8 14 us: layer_backward(): jnp.concatenate([grad_keys.reshape(batches, key_count, local_width), grad...]
    reduce_sum x13 -> x4, other arithmetic: 17.3 us -> 3.08 us  [layer_norm(): average = jnp.mean(values, axis=-1, keepdims=True)]
    reduce_sum x8 -> x5, other arithmetic: 15.2 us -> 3.35 us  [layer_norm(): return centered * lax.rsqrt(spread + EPSILON) * gains + biases]
  transfers between devices with their start and end apart: 22 -> 3, of which waited for: 17 -> 3; matrix products, arithmetic and copies ran while one was open for 10% -> 4% of each run, Pallas kernels for 0% -> 5%
where the time goes in v1:
time: 481 us; the launch traced here: 473 us
  Pallas kernels  201 us (42%)
  waiting for transfers between devices  101 us (21%)
  matrix products  48.1 us (10%)
  local copies, waits for them, and re-layouts  47.7 us (10%)
  other arithmetic  34.5 us (7%)
  blocking collectives  20.4 us (4%)
  between operations  15.6 us (3%)
    pallas_call x8, Pallas kernels, sum_tensor(): pl.pallas_call(functools.partial(sum_tensor_kernel, pieces), out_shape=ja...  91.9 us
    psum x1, waiting for transfers between devices, summed(): return lax.psum(member.astype(jnp.bfloat16), 'dp').astype(jnp.float32)  83.8 us
    pallas_call x2, Pallas kernels, scatter_dp(): pl.pallas_call(functools.partial(scatter_kernel, count), out_shape=jax.Sh...  63.3 us
    pallas_call x2, Pallas kernels, gather_dp(): pl.pallas_call(functools.partial(gather_kernel, count), out_shape=jax.Sha...  45.9 us
    psum x1, blocking collectives, layer_backward(): small = lax.psum(small, 'dp')  20.4 us
    ppermute x2, waiting for transfers between devices, passed_along(): return lax.ppermute(block, axis, route)  17 us
    concatenate x8, local copies, waits for them, and re-layouts, layer_backward(): jnp.concatenate([grad_keys.reshape(batches, key_count, local_width), grad...  14 us
    dot_general x7, matrix products, contract_cols(): lax.dot_general(left, right, (((1,), (1,)), ((), ())), preferred_element_...  10.7 us
  transfers between devices with their start and end apart: 3, of which 3 were waited for; matrix products, arithmetic and copies ran while one was open for 4% of the time, Pallas kernels for 5%

profile of v1, /device:TPU:0, one launch (start us, length us, event | category | flops | bytes accessed | tf_op | source)
XLA Modules:
  0.0 472.9 jit_solution(6223375456136710907)
XLA Ops:
  12.1 24.4 %shard_map.220 = bf16[4,3,128,384]{3,2,1,0:T(8,128)(2,1)S(1)} custom-call(bf16[3,128,384]{2,1,0:T(8,128)(2,1)S(1)} %bitcast.206), custom_call_target="tpu_custom_call" | custom-call | tf_op jit(solution)/shard_map/pallas_call | solution.py:222
  36.5 2.0 copy.36
  38.5 2.5 reshape.290
  42.2 3.6 fusion.179
  45.8 2.3 fusion.67
  48.7 11.7 %shard_map.221 = f32[384,768]{1,0:T(8,128)S(1)} custom-call(f32[384,768]{1,0:T(8,128)S(1)} %fusion.115.x_ref), custom_call_target="tpu_custom_call" | custom-call | tf_op jit(solution)/shard_map/pallas_call | solution.py:138
  61.6 1.6 multiply_reduce_fusion.10
  64.4 2.6 fusion.33.x_ref
  67.1 11.7 %shard_map.222 = f32[384,768]{1,0:T(8,128)S(1)} custom-call(f32[384,768]{1,0:T(8,128)S(1)} %fusion.33.x_ref), custom_call_target="tpu_custom_call" | custom-call | tf_op jit(solution)/shard_map/pallas_call | solution.py:138
  79.4 2.3 add_convert_fusion.4
  81.7 3.4 collective-permute-start
  85.2 13.4 %collective-permute-done = bf16[384,768]{1,0:T(8,128)(2,1)S(1)} collective-permute-done((bf16[384,768]{1,0:T(8,128)(2,1)}, bf16[384,768]{1,0:T(8,128)(2,1)S(1)}, u32[]{:S(2)}, u32[]{:S(2)}) %collective-permute-start) | collective-permute-done | bytes 589856 | tf_op jit(solution)/shard_map/ppermute | solution.py:25
  101.8 21.5 %shard_map.223 = bf16[4,3,128,384]{3,2,1,0:T(8,128)(2,1)S(1)} custom-call(bf16[3,128,384]{2,1,0:T(8,128)(2,1)S(1)} %bitcast.207), custom_call_target="tpu_custom_call" | custom-call | tf_op jit(solution)/shard_map/pallas_call | solution.py:222
  126.2 3.1 fusion.182
  129.3 2.2 fusion.66
  132.7 10.8 %shard_map.224 = f32[384,768]{1,0:T(8,128)S(1)} custom-call(f32[384,768]{1,0:T(8,128)S(1)} %fusion.113.x_ref), custom_call_target="tpu_custom_call" | custom-call | tf_op jit(solution)/shard_map/pallas_call | solution.py:138
  145.6 1.7 convolution_add_fusion
  147.3 3.7 fusion.37.x_ref
  151.0 11.7 %shard_map.226 = f32[384,768]{1,0:T(8,128)S(1)} custom-call(f32[384,768]{1,0:T(8,128)S(1)} %fusion.37.x_ref), custom_call_target="tpu_custom_call" | custom-call | tf_op jit(solution)/shard_map/pallas_call | solution.py:138
  165.7 1.6 reshape.296
  167.3 2.4 multiply_reduce_fusion.1
  176.6 2.3 concatenate.36
  178.9 2.2 copy.52
  181.1 1.6 maximum_bitcast_fusion.x_ref
  182.7 30.8 %shard_map.227 = f32[3,128,384]{2,1,0:T(8,128)S(1)} custom-call(bf16[4,3,128,384]{3,2,1,0:T(8,128)(2,1)S(1)} %maximum_bitcast_fusion.x_ref), custom_call_target="tpu_custom_call" | custom-call | tf_op jit(solution)/shard_map/pallas_call | solution.py:298
  214.2 11.7 %shard_map.228 = f32[384,768]{1,0:T(8,128)S(1)} custom-call(f32[384,768]{1,0:T(8,128)S(1)} %fusion.99.x_ref), custom_call_target="tpu_custom_call" | custom-call | tf_op jit(solution)/shard_map/pallas_call | solution.py:138
  230.3 11.7 %shard_map.225 = f32[384,768]{1,0:T(8,128)S(1)} custom-call(f32[384,768]{1,0:T(8,128)S(1)} %fusion.31.x_ref), custom_call_target="tpu_custom_call" | custom-call | tf_op jit(solution)/shard_map/pallas_call | solution.py:138
  242.1 3.6 collective-permute-done.1
  245.7 2.0 convert_reduce_fusion.1
  247.7 2.0 fusion.4
  250.3 10.9 %shard_map.229 = f32[384,768]{1,0:T(8,128)S(1)} custom-call(f32[384,768]{1,0:T(8,128)S(1)} %fusion.35.x_ref), custom_call_target="tpu_custom_call" | custom-call | tf_op jit(solution)/shard_map/pallas_call | solution.py:138
  266.7 1.6 reshape.298
  268.3 2.7 multiply_reduce_fusion
  272.3 1.8 convert_reduce_fusion.3
  280.2 2.3 concatenate.40
  282.4 2.2 copy.59
  284.6 1.6 maximum_bitcast_fusion.1.x_ref
  286.3 32.5 %shard_map.230 = f32[3,128,384]{2,1,0:T(8,128)S(1)} custom-call(bf16[4,3,128,384]{3,2,1,0:T(8,128)(2,1)S(1)} %maximum_bitcast_fusion.1.x_ref), custom_call_target="tpu_custom_call" | custom-call | tf_op jit(solution)/shard_map/pallas_call | solution.py:298
  318.8 1.8 convolution_convert_fusion.2
  320.7 2.1 fusion.5
  324.0 1.6 fusion.106.x_ref
  325.6 11.7 %shard_map.231 = f32[384,768]{1,0:T(8,128)S(1)} custom-call(f32[384,768]{1,0:T(8,128)S(1)} %fusion.106.x_ref), custom_call_target="tpu_custom_call" | custom-call | tf_op jit(solution)/shard_map/pallas_call | solution.py:138
  337.9 1.6 convert_reduce_fusion.2
  342.9 20.4 %psum.35 = f32[5760]{0:T(1024)} all-reduce(f32[5760]{0:T(1024)} %concatenate.43), channel_id=1, replica_groups=mesh['section'=2,'tensor'=4,'dp'=4] {'dp'}, use_global_device_ids=true, to_apply=%region_31.32 | all-reduce | flops 5760 | bytes 46080 | tf_op jit(solution)/shard_map/psum | solution.py:494
  372.4 2.6 add_add_fusion.4
  375.1 83.8 %all-reduce.3.cloned.1.call-done = (bf16[1,768,3,192]{1,3,2,0:T(8,128)(2,1)}, bf16[1,192,768]{2,1,0:T(8,128)(2,1)}, bf16[1,768,768]{2,1,0:T(8,128)(2,1)}, bf16[1,768,768]{2,1,0:T(8,128)(2,1)}) async-done(((bf16[1,768,3,192]{1,3,2,0:T(8,128)(2,1)}, bf16[1,192,768]{2,1,0:T(8,128)(2,1)}, bf16[1,768,768]{2,1,0:T(8,128)(2,1)}, bf16[1,768,768]{2,1,0:T(8,128)(2,1)}), (bf16[1,768,3,192]{1,3,2,0:T(8,128)(2,1)}, ...) | async-done | bytes 3538960 | tf_op jit(solution)/shard_map/psum | solution.py:421
  458.9 2.9 broadcast_in_dim.119
  461.8 1.6 broadcast_in_dim.122
  (275 shorter events, 63.5 us)
Async XLA Ops:
  7.2 57.3 %copy-start = (bf16[1,768,768]{2,1,0:T(8,128)(2,1)S(1)}, bf16[1,768,768]{2,1,0:T(8,128)(2,1)}, u32[]{:S(2)}) copy-start(bf16[1,768,768]{2,1,0:T(8,128)(2,1)} %param.23) | copy-start | bytes 3538948
  7.2 3.6 copy-start.5
  7.2 2.9 copy-start.83
  7.2 2.9 copy-start.76
  7.2 2.9 copy-start.75
  7.2 451.6 %all-reduce.3.cloned.1.call-start = ((), (), s32[]{:S(2)}) async-start(), calls=%async_computation | async-start | bytes 7077888 | tf_op jit(solution)/shard_map/psum | solution.py:421
  7.3 3.7 copy-start.9
  10.7 88.6 %copy-start.48 = (f32[768]{0:T(1024)}, f32[768]{0:T(1024)S(1)}, u32[]{:S(2)}) copy-start(f32[768]{0:T(1024)S(1)} %get-tuple-element.22) | copy-start | bytes 9220
  38.5 3.2 copy-start.74
  42.2 3.6 copy-start.45
  45.8 2.5 copy-start.21
  48.7 11.7 %copy-start.80 = (f32[1,768]{1,0:T(1,128)S(1)}, f32[1,768]{1,0:T(1,128)}, u32[]{:S(2)}) copy-start(f32[1,768]{1,0:T(1,128)} %param.20) | copy-start | bytes 9220
  61.6 2.2 copy-start.81
  61.6 2.8 copy-start.34
  67.1 11.7 %copy-start.82 = (f32[1,768]{1,0:T(1,128)S(1)}, f32[1,768]{1,0:T(1,128)}, u32[]{:S(2)}) copy-start(f32[1,768]{1,0:T(1,128)} %param.24) | copy-start | bytes 9220
  79.4 19.1 %copy-start.6 = (bf16[3,128,768]{2,1,0:T(8,128)(2,1)S(1)}, bf16[3,128,768]{2,1,0:T(8,128)(2,1)}, u32[]{:S(2)}) copy-start(bf16[3,128,768]{2,1,0:T(8,128)(2,1)} %param.13) | copy-start | bytes 1769476
  81.7 16.8 %collective-permute-start = (bf16[384,768]{1,0:T(8,128)(2,1)}, bf16[384,768]{1,0:T(8,128)(2,1)S(1)}, u32[]{:S(2)}, u32[]{:S(2)}) collective-permute-start(bf16[384,768]{1,0:T(8,128)(2,1)} %add_convert_fusion.4), channel_id=1, source_target_pairs={{0,16},{1,17},{2,18},{3,19},{4,20},{5,21},{6,22},{7,23},{8,24},{9,... | collective-permute-start | bytes 1769480 | tf_op jit(solution)/shard_map/ppermute | solution.py:25
  129.3 2.2 copy-start.13
  129.3 3.0 copy-start.22
  132.7 10.8 %copy-start.7 = (bf16[3,128,768]{2,1,0:T(8,128)(2,1)S(1)}, bf16[3,128,768]{2,1,0:T(8,128)(2,1)}, u32[]{:S(2)}) copy-start(bf16[3,128,768]{2,1,0:T(8,128)(2,1)} %param.13) | copy-start | bytes 1769476
  132.7 10.8 %copy-start.20 = (bf16[384,768]{1,0:T(8,128)(2,1)S(1)}, bf16[384,768]{1,0:T(8,128)(2,1)}, u32[]{:S(2)}) copy-start(bf16[384,768]{1,0:T(8,128)(2,1)} %copy-done.19) | copy-start | bytes 1769476
  132.7 10.8 %copy-start.53 = (f32[768]{0:T(1024)S(1)}, f32[768]{0:T(1024)}, u32[]{:S(2)}) copy-start(f32[768]{0:T(1024)} %copy-done.52) | copy-start | bytes 9220
  143.9 19.5 %copy-start.3 = (f32[384,768]{1,0:T(8,128)}, f32[384,768]{1,0:T(8,128)S(1)}, u32[]{:S(2)}) copy-start(f32[384,768]{1,0:T(8,128)S(1)} %get-tuple-element.34) | copy-start | bytes 3538948
  145.6 1.8 copy-start.57
  164.5 2.8 copy-start.25
  167.3 2.5 copy-start.14
  167.3 2.5 copy-start.63
  182.7 30.8 %copy-start.11 = (bf16[1,768,3,192]{1,3,2,0:T(8,128)(2,1)S(1)}, bf16[1,768,3,192]{1,3,2,0:T(8,128)(2,1)}, u32[]{:S(2)}) copy-start(bf16[1,768,3,192]{1,3,2,0:T(8,128)(2,1)} %param.17) | copy-start | bytes 2654212
  214.2 11.7 %copy-start.2 = (f32[384,768]{1,0:T(8,128)S(1)}, f32[384,768]{1,0:T(8,128)}, u32[]{:S(2)}) copy-start(f32[384,768]{1,0:T(8,128)} %copy-done.1) | copy-start | bytes 3538948
  227.7 1.8 copy-start.84
  228.2 17.5 %collective-permute-start.1 = (bf16[384,768]{1,0:T(8,128)(2,1)S(1)}, bf16[384,768]{1,0:T(8,128)(2,1)S(1)}, u32[]{:S(2)}, u32[]{:S(2)}) collective-permute-start(bf16[384,768]{1,0:T(8,128)(2,1)S(1)} %add_convert_fusion), channel_id=1, source_target_pairs={{16,0},{17,1},{18,2},{19,3},{20,4},{21,5},{22,6},{23,7},{24,8},{25... | collective-permute-start | bytes 1769480 | tf_op jit(solution)/shard_map/ppermute | solution.py:25
  242.1 5.6 %copy-start.4 = (f32[384,768]{1,0:T(8,128)S(1)}, f32[384,768]{1,0:T(8,128)}, u32[]{:S(2)}) copy-start(f32[384,768]{1,0:T(8,128)} %copy-done.3) | copy-start | bytes 3538948
  242.1 5.6 %copy-start.59 = (f32[384]{0:T(512)S(1)}, f32[384]{0:T(512)}, u32[]{:S(2)}) copy-start(f32[384]{0:T(512)} %copy-done.57) | copy-start | bytes 4612
  242.1 5.6 %copy-start.78 = (f32[768]{0:T(1024)S(1)}, f32[768]{0:T(1024)}, u32[]{:S(2)}) copy-start(f32[768]{0:T(1024)} %get-tuple-element.21) | copy-start | bytes 9220
  245.7 17.9 %copy-start.39 = (bf16[384,768]{1,0:T(8,128)(2,1)}, bf16[384,768]{1,0:T(8,128)(2,1)S(1)}, u32[]{:S(2)}) copy-start(bf16[384,768]{1,0:T(8,128)(2,1)S(1)} %collective-permute-done.1) | copy-start | bytes 1769476
  247.7 2.0 copy-start.36
  264.5 6.5 %copy-start.8 = (f32[384,768]{1,0:T(8,128)}, f32[384,768]{1,0:T(8,128)S(1)}, u32[]{:S(2)}) copy-start(f32[384,768]{1,0:T(8,128)S(1)} %get-tuple-element.28) | copy-start | bytes 3538948
  265.6 2.7 copy-start.64
  268.3 2.7 copy-start.15
  272.3 1.8 copy-start.32
  286.2 32.6 %copy-start.38 = (bf16[384,192]{1,0:T(8,128)(2,1)S(1)}, bf16[384,192]{1,0:T(8,128)(2,1)}, u32[]{:S(2)}) copy-start(bf16[384,192]{1,0:T(8,128)(2,1)} %reshape.304) | copy-start | bytes 442372
  286.2 32.6 %copy-start.49 = (f32[768]{0:T(1024)S(1)}, f32[768]{0:T(1024)}, u32[]{:S(2)}) copy-start(f32[768]{0:T(1024)} %copy-done.48) | copy-start | bytes 9220
  318.8 4.0 copy-start.28
  318.8 1.9 copy-start.18
  318.8 1.9 copy-start.40
  318.8 1.9 copy-start.85
  325.6 11.7 %copy-start.73 = (f32[3,64]{1,0:T(4,128)S(1)}, f32[3,64]{1,0:T(4,128)}, u32[]{:S(2)}) copy-start(f32[3,64]{1,0:T(4,128)} %get-tuple-element.60) | copy-start | bytes 2308
  458.9 2.9 copy-start.33
  (41 other events, 45.2 us)
Sparse Core Ops, SparseCore 0:
  322.9 135.8 all-reduce.2

commit v2 on v1

--- a/solution.py
+++ b/solution.py
@@ -17,12 +17,6 @@
 GELU_CUBE = 0.044715
 MESH = pl.DeviceIdType.MESH
 VMEM_BYTES = 48 * 1024 * 1024
-
-
-def passed_along(block, axis, distance):
-    devices = range(lax.axis_size(axis))
-    route = [(i - distance, i) for i in devices if i - distance in devices]
-    return lax.ppermute(block, axis, route)
 
 
 def layer_norm(values, gains, biases):
@@ -148,6 +142,64 @@
     )(partial)
 
 
+def swap_kernel(pieces, x_ref, o_ref, send, recv):
+    section = lax.axis_index("section")
+    me = lax.axis_index("tensor")
+    parity = lax.rem(me, 2)
+    near = me + 1 - 2 * parity
+    half = x_ref.shape[0] // 2
+    rows = half // pieces
+    barrier = pltpu.get_barrier_semaphore()
+    pl.semaphore_signal(
+        barrier, inc=1, device_id={"section": 1 - section}, device_id_type=MESH
+    )
+    pl.semaphore_signal(barrier, inc=1, device_id={"tensor": near}, device_id_type=MESH)
+    pl.semaphore_wait(barrier, 2)
+
+    def copy(source, step, k, owner, device):
+        span = pl.ds(pl.multiple_of(owner * half + k * rows, 16), rows)
+        return pltpu.make_async_remote_copy(
+            src_ref=source.at[span],
+            dst_ref=o_ref.at[span],
+            send_sem=send.at[step, k],
+            recv_sem=recv.at[step, k],
+            device_id=device,
+            device_id_type=MESH,
+        )
+
+    across = [copy(x_ref, 0, k, parity, {"section": 1 - section}) for k in range(pieces)]
+    beside = [copy(o_ref, 1, k, parity, {"tensor": near}) for k in range(pieces)]
+    arriving = [copy(o_ref, 1, k, 1 - parity, {"tensor": near}) for k in range(pieces)]
+    for k in range(pieces):
+        across[k].start()
+    for k in range(pieces):
+        across[k].wait_recv()
+        beside[k].start()
+    for k in range(pieces):
+        arriving[k].wait_recv()
+        across[k].wait_send()
+        beside[k].wait_send()
+
+
+def swap_sections(block):
+    pieces = 3
+    if lax.axis_size("section") != 2 or lax.axis_size("tensor") % 2 or block.shape[0] % 96:
+        return lax.ppermute(block, "section", [(0, 1), (1, 0)])
+    return pl.pallas_call(
+        functools.partial(swap_kernel, pieces),
+        out_shape=jax.ShapeDtypeStruct(block.shape, block.dtype),
+        in_specs=[pl.BlockSpec(memory_space=pltpu.VMEM)],
+        out_specs=pl.BlockSpec(memory_space=pltpu.VMEM),
+        scratch_shapes=[
+            pltpu.SemaphoreType.DMA((2, pieces)),
+            pltpu.SemaphoreType.DMA((2, pieces)),
+        ],
+        compiler_params=pltpu.CompilerParams(
+            collective_id=3, has_side_effects=True, vmem_limit_bytes=VMEM_BYTES
+        ),
+    )(block)
+
+
 def gather_kernel(count, x_ref, o_ref, send, recv):
     me = lax.axis_index("dp")
     batches = x_ref.shape[0]
@@ -250,25 +302,30 @@
         for m in range(batches):
             for side in range(2):
                 owner = count - 1 - step if side == 0 else step
-                at_end = me == 0 if side == 0 else me == count - 1
-                inside = (
-                    jnp.logical_and(me > 0, me < owner)
-                    if side == 0
-                    else jnp.logical_and(me < count - 1, me > owner)
-                )
-
-                @pl.when(at_end)
+
+                @pl.when(me == 0 if side == 0 else me == count - 1)
                 def _():
                     copy(side, step, m, x_ref.at[owner, m]).start()
 
-                @pl.when(inside)
-                def _():
-                    copy(side, step, m, landed.at[side, step, m]).wait_recv()
-                    landed[side, step, m] = (
-                        landed[side, step, m].astype(jnp.float32)
-                        + x_ref[owner, m].astype(jnp.float32)
-                    ).astype(jnp.bfloat16)
-                    copy(side, step, m, landed.at[side, step, m]).start()
+    items = (count - 1) * batches
+    for slot in range(1, items + count - 2):
+        for side in range(2):
+            item = slot - (me if side == 0 else count - 1 - me)
+            step = lax.div(item, batches)
+            m = item - step * batches
+            owner = count - 1 - step if side == 0 else step
+            moves = me < owner if side == 0 else me > owner
+            inner = me > 0 if side == 0 else me < count - 1
+            valid = jnp.logical_and(item >= 0, item < items)
+
+            @pl.when(jnp.logical_and(jnp.logical_and(inner, valid), moves))
+            def _():
+                copy(side, step, m, landed.at[side, step, m]).wait_recv()
+                landed[side, step, m] = (
+                    landed[side, step, m].astype(jnp.float32)
+                    + x_ref[owner, m].astype(jnp.float32)
+                ).astype(jnp.bfloat16)
+                copy(side, step, m, landed.at[side, step, m]).start()
 
     for m in range(batches):
         o_ref[m] = x_ref[me, m].astype(jnp.float32)
@@ -417,16 +474,13 @@
     key_count = key_heads.shape[1]
     score_scale = 1.0 / math.sqrt(HEAD)
 
-    def summed(member):
-        return lax.psum(member.astype(jnp.bfloat16), "dp").astype(jnp.float32)
-
     grad_low = grad_output.astype(jnp.bfloat16)
     grad_active = contract_cols(grad_low, proj_weight)
     grad_pre = jax.vjp(gelu_tanh, hidden_pre)[1](grad_active)[0].astype(jnp.bfloat16)
     grad_normed_mid = sum_tensor(contract_cols(grad_pre, fc_weight))
     if with_grads:
-        grad_proj_weight = summed(contract_rows(active, grad_low))
-        grad_fc_weight = summed(contract_rows(normed_mid, grad_pre))
+        grad_proj_weight = contract_rows(active, grad_low).astype(jnp.bfloat16)
+        grad_fc_weight = contract_rows(normed_mid, grad_pre).astype(jnp.bfloat16)
     grad_middle_norm, grad_gain_mid, grad_bias_mid = jax.vjp(
         layer_norm, middle, gains[1], biases[1]
     )[1](grad_normed_mid)
@@ -434,7 +488,8 @@
     middle_low = grad_middle.astype(jnp.bfloat16)
     grad_attended = contract_cols(middle_low, out_weight).astype(jnp.bfloat16)
     if with_grads:
-        grad_out_weight = summed(contract_rows(attended, middle_low))
+        grad_out_weight = contract_rows(attended, middle_low).astype(jnp.bfloat16)
+        early = lax.psum((grad_proj_weight, grad_fc_weight, grad_out_weight), "dp")
     grad_heads = grad_attended.reshape(batches, shard_rows, head_count, HEAD)
     grad_softmax = jnp.einsum(
         "mqhe,mkhe->mhqk", grad_heads, value_heads, preferred_element_type=jnp.float32
@@ -470,7 +525,7 @@
     grad_projected = jnp.concatenate([grad_query, grad_keys, grad_values], axis=1)
     qkv_flat = qkv_weight.reshape(qkv_weight.shape[0], -1)
     if with_grads:
-        grad_qkv_weight = summed(contract_rows(normed, grad_projected)).reshape(qkv_weight.shape)
+        grad_qkv_weight = contract_rows(normed, grad_projected).astype(jnp.bfloat16)
     grad_normed = sum_tensor(contract_cols(grad_projected, qkv_flat))
     grad_input_norm, grad_gain_in, grad_bias_in = jax.vjp(layer_norm, inputs, gains[0], biases[0])[
         1
@@ -490,8 +545,18 @@
             jnp.sum(grad_pre.astype(jnp.float32), axis=0),
             jnp.sum(grad_output, axis=0),
         ]
-    )
-    small = lax.psum(small, "dp")
+    ).astype(jnp.bfloat16)
+    columns = 3 * local_width
+    small_rows = -(-small.shape[0] // columns)
+    small = jnp.pad(small, (0, small_rows * columns - small.shape[0]))
+    late = jnp.concatenate([grad_qkv_weight, small.reshape(small_rows, columns)], axis=0)
+    late, early = lax.optimization_barrier((late, early))
+    late = lax.psum(late, "dp").astype(jnp.float32)
+    grad_proj_weight, grad_fc_weight, grad_out_weight = (
+        member.astype(jnp.float32) for member in early
+    )
+    grad_qkv_weight = late[: qkv_weight.shape[0]]
+    small = late[qkv_weight.shape[0] :].reshape(-1)
     width = gains.shape[1]
     sizes = (2 * width, 2 * width, 2 * local_width, width, fc_bias.shape[0], width)
     parts = []
@@ -502,7 +567,7 @@
     grads = (
         parts[0].reshape(gains.shape),
         parts[1].reshape(biases.shape),
-        grad_qkv_weight,
+        grad_qkv_weight.reshape(qkv_weight.shape),
         parts[2].reshape(qv_bias.shape),
         grad_out_weight,
         parts[3],
@@ -552,12 +617,12 @@
     rows = micro_count * shard_rows
     inputs = tokens.reshape(rows, model_width).astype(jnp.float32)
     output, _ = layer_forward(inputs, allowed, params)
-    received = passed_along(output.astype(jnp.bfloat16), "section", 1).astype(jnp.float32)
+    received = swap_sections(output.astype(jnp.bfloat16)).astype(jnp.float32)
     inputs = jnp.where(is_first, inputs, received)
     output, saved_state = layer_forward(inputs, allowed, params)
     seed_grad = cotangent.reshape(rows, model_width).astype(jnp.float32)
     grad_input, _ = layer_backward(seed_grad, saved_state, params, False)
-    received = passed_along(grad_input.astype(jnp.bfloat16), "section", -1).astype(jnp.float32)
+    received = swap_sections(grad_input.astype(jnp.bfloat16)).astype(jnp.float32)
     grad_output = jnp.where(is_first, received, seed_grad)
     grad_input, grads = layer_backward(grad_output, saved_state, params, True)
     section_out = output.astype(jnp.bfloat16).reshape(tokens.shape)[None]

time: 481 us -> 461 us (0.958)
  waiting for transfers between devices: 101 us -> 72.7 us
  blocking collectives: 20.4 us -> 0 us
  Pallas kernels: 201 us -> 221 us
  local copies, waits for them, and re-layouts: 47.7 us -> 59.7 us
    pallas_call x0 -> x2, Pallas kernels: none -> 20.8 us  [swap_sections(): pl.pallas_call(functools.partial(swap_kernel, pieces), out_shape=jax.Shap...]
    psum x1 -> x0, blocking collectives: 20.4 us -> none  [layer_backward(): small = lax.psum(small, 'dp')]
    ppermute x2 -> x0, waiting for transfers between devices: 17 us -> none  [passed_along(): return lax.ppermute(block, axis, route)]
    psum x1 -> x2, waiting for transfers between devices: 83.8 us -> 72.6 us  [the longest x1 46.1 us: layer_backward(): late = lax.psum(late, 'dp').astype(jnp.float32)]
    concatenate x1, local copies, waits for them, and re-layouts: 1.45 us -> 6.74 us  [layer_backward(): jnp.concatenate([grad_gain_in, grad_gain_mid, grad_bias_in, grad_bias_mid...]
  transfers between devices with their start and end apart: 3 -> 2, of which waited for: 3 -> 2; matrix products, arithmetic and copies ran while one was open for 4% -> 11% of each run, Pallas kernels for 5% -> 11%
where the time goes in v2:
time: 461 us; the launch traced here: 452 us
  Pallas kernels  221 us (48%)
  waiting for transfers between devices  72.7 us (16%)
  local copies, waits for them, and re-layouts  59.7 us (13%)
  matrix products  51.3 us (11%)
  other arithmetic  32 us (7%)
  between operations  15.6 us (3%)
    pallas_call x8, Pallas kernels, sum_tensor(): pl.pallas_call(functools.partial(sum_tensor_kernel, pieces), out_shape=ja...  92.7 us
    pallas_call x2, Pallas kernels, scatter_dp(): pl.pallas_call(functools.partial(scatter_kernel, count), out_shape=jax.Sh...  60.5 us
    pallas_call x2, Pallas kernels, gather_dp(): pl.pallas_call(functools.partial(gather_kernel, count), out_shape=jax.Sha...  46.7 us
    psum x1, waiting for transfers between devices, layer_backward(): late = lax.psum(late, 'dp').astype(jnp.float32)  46.1 us
    psum x1, waiting for transfers between devices, layer_backward(): early = lax.psum((grad_proj_weight, grad_fc_weight, grad_out_weight), 'dp')  26.5 us
    pallas_call x2, Pallas kernels, swap_sections(): pl.pallas_call(functools.partial(swap_kernel, pieces), out_shape=jax.Shap...  20.8 us
    concatenate x8, local copies, waits for them, and re-layouts, layer_backward(): jnp.concatenate([grad_keys.reshape(batches, key_count, local_width), grad...  15.4 us
    dot_general x7, matrix products, contract_cols(): lax.dot_general(left, right, (((1,), (1,)), ((), ())), preferred_element_...  10.7 us
  transfers between devices with their start and end apart: 2, of which 2 were waited for; matrix products, arithmetic and copies ran while one was open for 11% of the time, Pallas kernels for 11%

profile of v2, /device:TPU:0, one launch (start us, length us, event | category | flops | bytes accessed | tf_op | source)
XLA Modules:
  0.0 452.3 jit_solution(15101014246051378290)
XLA Ops:
  12.1 24.4 %shard_map.220 = bf16[4,3,128,384]{3,2,1,0:T(8,128)(2,1)S(1)} custom-call(bf16[3,128,384]{2,1,0:T(8,128)(2,1)S(1)} %bitcast.209), custom_call_target="tpu_custom_call" | custom-call | tf_op jit(solution)/shard_map/pallas_call | solution.py:274
  36.5 2.0 copy.36
  38.5 2.5 reshape.291
  42.2 3.6 fusion.176
  45.8 2.3 fusion.64
  48.7 11.7 %shard_map.221 = f32[384,768]{1,0:T(8,128)S(1)} custom-call(f32[384,768]{1,0:T(8,128)S(1)} %fusion.112.x_ref), custom_call_target="tpu_custom_call" | custom-call | tf_op jit(solution)/shard_map/pallas_call | solution.py:132
  61.6 1.6 multiply_reduce_fusion.10
  64.4 2.6 fusion.31.x_ref
  67.1 11.7 %shard_map.222 = f32[384,768]{1,0:T(8,128)S(1)} custom-call(f32[384,768]{1,0:T(8,128)S(1)} %fusion.31.x_ref), custom_call_target="tpu_custom_call" | custom-call | tf_op jit(solution)/shard_map/pallas_call | solution.py:132
  80.9 10.4 %shard_map.223 = bf16[384,768]{1,0:T(8,128)(2,1)S(1)} custom-call(bf16[384,768]{1,0:T(8,128)(2,1)S(1)} %add_convert_fusion.4.x_ref), custom_call_target="tpu_custom_call" | custom-call | tf_op jit(solution)/shard_map/pallas_call | solution.py:188
  93.9 22.3 %shard_map.224 = bf16[4,3,128,384]{3,2,1,0:T(8,128)(2,1)S(1)} custom-call(bf16[3,128,384]{2,1,0:T(8,128)(2,1)S(1)} %bitcast.210), custom_call_target="tpu_custom_call" | custom-call | tf_op jit(solution)/shard_map/pallas_call | solution.py:274
  116.3 2.2 copy.42
  118.4 2.5 reshape.294
  121.0 4.0 fusion.179
  125.0 2.3 fusion.63
  128.5 10.8 %shard_map.225 = f32[384,768]{1,0:T(8,128)S(1)} custom-call(f32[384,768]{1,0:T(8,128)S(1)} %fusion.110.x_ref), custom_call_target="tpu_custom_call" | custom-call | tf_op jit(solution)/shard_map/pallas_call | solution.py:132
  141.4 1.7 convolution_add_fusion
  143.2 3.7 fusion.35.x_ref
  146.8 11.7 %shard_map.227 = f32[384,768]{1,0:T(8,128)S(1)} custom-call(f32[384,768]{1,0:T(8,128)S(1)} %fusion.35.x_ref), custom_call_target="tpu_custom_call" | custom-call | tf_op jit(solution)/shard_map/pallas_call | solution.py:132
  161.5 1.6 reshape.297
  163.2 2.4 multiply_reduce_fusion.1
  173.4 2.3 concatenate.40
  175.7 2.2 copy.52
  179.5 20.3 %shard_map.228 = f32[3,128,384]{2,1,0:T(8,128)S(1)} custom-call(bf16[4,3,128,384]{3,2,1,0:T(8,128)(2,1)S(1)} %maximum_bitcast_fusion.x_ref), custom_call_target="tpu_custom_call" | custom-call | tf_op jit(solution)/shard_map/pallas_call | solution.py:355
  200.6 11.7 %shard_map.229 = f32[384,768]{1,0:T(8,128)S(1)} custom-call(f32[384,768]{1,0:T(8,128)S(1)} %fusion.96.x_ref), custom_call_target="tpu_custom_call" | custom-call | tf_op jit(solution)/shard_map/pallas_call | solution.py:132
  214.9 10.4 %shard_map.230 = bf16[384,768]{1,0:T(8,128)(2,1)S(1)} custom-call(bf16[384,768]{1,0:T(8,128)(2,1)S(1)} %add_convert_fusion.x_ref), custom_call_target="tpu_custom_call" | custom-call | tf_op jit(solution)/shard_map/pallas_call | solution.py:188
  225.3 2.0 fusion.183
  228.5 2.0 convolution_convert_fusion
  230.5 2.1 convolution_convert_fusion.1
  232.6 11.7 %shard_map.231 = f32[384,768]{1,0:T(8,128)S(1)} custom-call(f32[384,768]{1,0:T(8,128)S(1)} %fusion.33.x_ref), custom_call_target="tpu_custom_call" | custom-call | tf_op jit(solution)/shard_map/pallas_call | solution.py:132
  245.3 11.7 %shard_map.226 = f32[384,768]{1,0:T(8,128)S(1)} custom-call(f32[384,768]{1,0:T(8,128)S(1)} %fusion.29.x_ref), custom_call_target="tpu_custom_call" | custom-call | tf_op jit(solution)/shard_map/pallas_call | solution.py:132
  260.7 2.0 convolution_convert_fusion.6
  264.3 2.7 multiply_reduce_fusion
  269.8 1.9 copy.65
  271.7 1.9 reshape.309
  273.6 2.1 fusion.8
  275.7 2.3 concatenate.43
  279.6 2.9 fusion.7
  282.5 2.3 concatenate.44
  284.8 2.2 copy.59
  288.6 40.1 %shard_map.232 = f32[3,128,384]{2,1,0:T(8,128)S(1)} custom-call(bf16[4,3,128,384]{3,2,1,0:T(8,128)(2,1)S(1)} %maximum_bitcast_fusion.1.x_ref), custom_call_target="tpu_custom_call" | custom-call | tf_op jit(solution)/shard_map/pallas_call | solution.py:355
  330.2 11.7 %shard_map.233 = f32[384,768]{1,0:T(8,128)S(1)} custom-call(f32[384,768]{1,0:T(8,128)S(1)} %fusion.103.x_ref), custom_call_target="tpu_custom_call" | custom-call | tf_op jit(solution)/shard_map/pallas_call | solution.py:132
  342.5 1.7 slice_reduce_fusion
  346.0 6.7 %concatenate.47 = bf16[5760]{0:T(1024)(128)(2,1)} concatenate(bf16[768]{0:T(1024)(128)(2,1)} %get-tuple-element.22, bf16[768]{0:T(1024)(128)(2,1)} %get-tuple-element.20, bf16[768]{0:T(1024)(128)(2,1)} %get-tuple-element.25, bf16[768]{0:T(1024)(128)(2,1)} %get-tuple-element.24, bf16[192]{0:T(256)(128)(2,1)} %reduce_sum.301, bf16[192]{0:T(256)(128)(2,1)} %slice_reduce_fusion, ...), dimensions={0} | concatenate | bytes 23040 | tf_op jit(solution)/shard_map/concatenate | solution.py:536
  355.6 2.0 convolution_convert_fusion.2
  359.3 26.5 %all-reduce.6.cloned.1.call-done = (bf16[768,768]{1,0:T(8,128)(2,1)}, bf16[768,768]{1,0:T(8,128)(2,1)}, bf16[192,768]{1,0:T(8,128)(2,1)}) async-done(((bf16[768,768]{1,0:T(8,128)(2,1)}, bf16[768,768]{1,0:T(8,128)(2,1)}, bf16[192,768]{1,0:T(8,128)(2,1)}), (bf16[768,768]{1,0:T(8,128)(2,1)}, bf16[768,768]{1,0:T(8,128)(2,1)}, bf16[192,768]{1,0:T(8,128)(2,1)})) %all-reduce.6.cloned.1.call-update) | async-done | bytes 2654224 | tf_op jit(solution)/shard_map/psum | solution.py:492
  385.8 2.7 add_add_fusion.4
  392.7 46.1 %all-reduce.4.cloned.1.call-done = bf16[778,576]{0,1:T(8,128)(2,1)} async-done(((bf16[778,576]{0,1:T(8,128)(2,1)}), bf16[778,576]{0,1:T(8,128)(2,1)}) %all-reduce.4.cloned.1.call-update) | async-done | bytes 896272 | tf_op jit(solution)/shard_map/psum | solution.py:554
  (269 shorter events, 64.4 us)
Async XLA Ops:
  7.2 57.2 %copy-start = (bf16[1,768,768]{2,1,0:T(8,128)(2,1)S(1)}, bf16[1,768,768]{2,1,0:T(8,128)(2,1)}, u32[]{:S(2)}) copy-start(bf16[1,768,768]{2,1,0:T(8,128)(2,1)} %param.23) | copy-start | bytes 3538948
  7.2 3.5 copy-start.5
  7.2 2.9 copy-start.77
  7.2 2.9 copy-start.71
  7.2 2.9 copy-start.70
  7.2 378.5 %all-reduce.6.cloned.1.call-start = ((), (), s32[]{:S(2)}) async-start(), calls=%async_computation.1 | async-start | bytes 5308416 | tf_op jit(solution)/shard_map/psum | solution.py:492
  7.3 3.7 copy-start.9
  10.7 81.2 %copy-start.43 = (f32[768]{0:T(1024)}, f32[768]{0:T(1024)S(1)}, u32[]{:S(2)}) copy-start(f32[768]{0:T(1024)S(1)} %get-tuple-element.30) | copy-start | bytes 9220
  38.5 3.2 copy-start.69
  42.2 3.6 copy-start.40
  45.8 2.5 copy-start.19
  48.6 11.7 %copy-start.75 = (f32[1,768]{1,0:T(1,128)S(1)}, f32[1,768]{1,0:T(1,128)}, u32[]{:S(2)}) copy-start(f32[1,768]{1,0:T(1,128)} %param.20) | copy-start | bytes 9220
  61.6 2.2 copy-start.76
  61.6 2.8 copy-start.33
  80.9 10.4 %copy-start.6 = (bf16[3,128,768]{2,1,0:T(8,128)(2,1)S(1)}, bf16[3,128,768]{2,1,0:T(8,128)(2,1)}, u32[]{:S(2)}) copy-start(bf16[3,128,768]{2,1,0:T(8,128)(2,1)} %param.13) | copy-start | bytes 1769476
  120.9 4.1 copy-start.22
  121.0 4.0 copy-start.29
  125.0 2.3 copy-start.58
  125.0 3.1 copy-start.20
  128.5 10.9 %copy-start.7 = (bf16[3,128,768]{2,1,0:T(8,128)(2,1)S(1)}, bf16[3,128,768]{2,1,0:T(8,128)(2,1)}, u32[]{:S(2)}) copy-start(bf16[3,128,768]{2,1,0:T(8,128)(2,1)} %param.13) | copy-start | bytes 1769476
  128.5 10.9 %copy-start.48 = (f32[768]{0:T(1024)S(1)}, f32[768]{0:T(1024)}, u32[]{:S(2)}) copy-start(f32[768]{0:T(1024)} %copy-done.47) | copy-start | bytes 9220
  139.7 19.5 %copy-start.3 = (f32[384,768]{1,0:T(8,128)}, f32[384,768]{1,0:T(8,128)S(1)}, u32[]{:S(2)}) copy-start(f32[384,768]{1,0:T(8,128)S(1)} %get-tuple-element.41) | copy-start | bytes 3538948
  139.7 1.7 copy-start.34
  139.7 1.7 copy-start.72
  139.7 1.7 copy-start.74
  141.4 1.8 copy-start.52
  159.7 3.4 copy-start.13
  160.4 2.8 copy-start.23
  163.2 2.5 copy-start.15
  163.2 2.5 copy-start.59
  179.5 20.4 %copy-start.11 = (bf16[1,768,3,192]{1,3,2,0:T(8,128)(2,1)S(1)}, bf16[1,768,3,192]{1,3,2,0:T(8,128)(2,1)}, u32[]{:S(2)}) copy-start(bf16[1,768,3,192]{1,3,2,0:T(8,128)(2,1)} %param.17) | copy-start | bytes 2654212
  200.6 11.7 %copy-start.2 = (f32[384,768]{1,0:T(8,128)S(1)}, f32[384,768]{1,0:T(8,128)}, u32[]{:S(2)}) copy-start(f32[384,768]{1,0:T(8,128)} %copy-done.1) | copy-start | bytes 3538948
  214.4 10.9 %copy-start.79 = (f32[384,768]{1,0:T(8,128)S(1)}, f32[384,768]{1,0:T(8,128)}, u32[]{:S(2)}) copy-start(f32[384,768]{1,0:T(8,128)} %convolution_add_fusion) | copy-start | bytes 3538948
  225.3 2.0 copy-start.35
  245.3 11.7 %copy-start.46 = (f32[768]{0:T(1024)S(1)}, f32[768]{0:T(1024)}, u32[]{:S(2)}) copy-start(f32[768]{0:T(1024)} %copy-done.45) | copy-start | bytes 9220
  259.3 7.7 %copy-start.8 = (f32[384,768]{1,0:T(8,128)}, f32[384,768]{1,0:T(8,128)S(1)}, u32[]{:S(2)}) copy-start(f32[384,768]{1,0:T(8,128)S(1)} %get-tuple-element.35) | copy-start | bytes 3538948
  260.4 178.4 %all-reduce.4.cloned.1.call-start = ((), (), s32[]{:S(2)}) async-start(), calls=%async_computation | async-start | bytes 2064384 | tf_op jit(solution)/shard_map/psum | solution.py:554
  264.3 3.0 copy-start.16
  264.3 3.0 copy-start.60
  275.7 3.9 copy-start.41
  275.7 3.9 copy-start.61
  288.6 40.9 %copy-start.12 = (bf16[1,768,3,192]{1,3,2,0:T(8,128)(2,1)S(1)}, bf16[1,768,3,192]{1,3,2,0:T(8,128)(2,1)}, u32[]{:S(2)}) copy-start(bf16[1,768,3,192]{1,3,2,0:T(8,128)(2,1)} %param.17) | copy-start | bytes 2654212
  288.6 40.9 %copy-start.36 = (bf16[384,192]{1,0:T(8,128)(2,1)S(1)}, bf16[384,192]{1,0:T(8,128)(2,1)}, u32[]{:S(2)}) copy-start(bf16[384,192]{1,0:T(8,128)(2,1)} %reshape.309) | copy-start | bytes 442372
  344.9 10.8 %copy-start.44 = (f32[768]{0:T(1024)S(1)}, f32[768]{0:T(1024)}, u32[]{:S(2)}) copy-start(f32[768]{0:T(1024)} %copy-done.43) | copy-start | bytes 9220
  355.6 2.0 copy-start.37
  385.8 2.8 copy-start.39
  385.8 3.6 copy-start.32
  438.8 4.9 %copy-start.25 = (bf16[778,576]{0,1:T(8,128)(2,1)S(1)}, bf16[778,576]{0,1:T(8,128)(2,1)}, u32[]{:S(2)}) copy-start(bf16[778,576]{0,1:T(8,128)(2,1)} %all-reduce.4.cloned.1.call-done) | copy-start | bytes 2688772
  (34 other events, 37.5 us)
Sparse Core Ops, SparseCore 0:
  260.5 125.2 all-reduce.5
  388.1 50.6 all-reduce.3

commit v3 on v2

--- a/solution.py
+++ b/solution.py
@@ -477,10 +477,15 @@
     grad_low = grad_output.astype(jnp.bfloat16)
     grad_active = contract_cols(grad_low, proj_weight)
     grad_pre = jax.vjp(gelu_tanh, hidden_pre)[1](grad_active)[0].astype(jnp.bfloat16)
-    grad_normed_mid = sum_tensor(contract_cols(grad_pre, fc_weight))
+    partial_mid = contract_cols(grad_pre, fc_weight)
     if with_grads:
         grad_proj_weight = contract_rows(active, grad_low).astype(jnp.bfloat16)
         grad_fc_weight = contract_rows(normed_mid, grad_pre).astype(jnp.bfloat16)
+        partial_mid, grad_proj_weight, grad_fc_weight = lax.optimization_barrier(
+            (partial_mid, grad_proj_weight, grad_fc_weight)
+        )
+        early = lax.psum((grad_proj_weight, grad_fc_weight), "dp")
+    grad_normed_mid = sum_tensor(partial_mid)
     grad_middle_norm, grad_gain_mid, grad_bias_mid = jax.vjp(
         layer_norm, middle, gains[1], biases[1]
     )[1](grad_normed_mid)
@@ -489,7 +494,6 @@
     grad_attended = contract_cols(middle_low, out_weight).astype(jnp.bfloat16)
     if with_grads:
         grad_out_weight = contract_rows(attended, middle_low).astype(jnp.bfloat16)
-        early = lax.psum((grad_proj_weight, grad_fc_weight, grad_out_weight), "dp")
     grad_heads = grad_attended.reshape(batches, shard_rows, head_count, HEAD)
     grad_softmax = jnp.einsum(
         "mqhe,mkhe->mhqk", grad_heads, value_heads, preferred_element_type=jnp.float32
@@ -550,11 +554,11 @@
     small_rows = -(-small.shape[0] // columns)
     small = jnp.pad(small, (0, small_rows * columns - small.shape[0]))
     late = jnp.concatenate([grad_qkv_weight, small.reshape(small_rows, columns)], axis=0)
-    late, early = lax.optimization_barrier((late, early))
-    late = lax.psum(late, "dp").astype(jnp.float32)
-    grad_proj_weight, grad_fc_weight, grad_out_weight = (
-        member.astype(jnp.float32) for member in early
-    )
+    late, grad_out_weight, early = lax.optimization_barrier((late, grad_out_weight, early))
+    late, grad_out_weight = lax.psum((late, grad_out_weight), "dp")
+    late = late.astype(jnp.float32)
+    grad_out_weight = grad_out_weight.astype(jnp.float32)
+    grad_proj_weight, grad_fc_weight = (member.astype(jnp.float32) for member in early)
     grad_qkv_weight = late[: qkv_weight.shape[0]]
     small = late[qkv_weight.shape[0] :].reshape(-1)
     width = gains.shape[1]

time: 461 us -> 433 us (0.939)
  local copies, waits for them, and re-layouts: 59.7 us -> 48.9 us
  waiting for transfers between devices: 72.7 us -> 62.7 us
    psum x2, waiting for transfers between devices: 72.6 us -> 62.7 us  [the longest x1 62.7 us: layer_backward(): late, grad_out_weight = lax.psum((late, grad_out_weight), 'dp')]
    concatenate x8, local copies, waits for them, and re-layouts: 15.4 us -> 7.92 us  [layer_backward(): jnp.concatenate([grad_keys.reshape(batches, key_count, local_width), grad...]
    unnamed x161 -> x159, local copies, waits for them, and re-layouts: 9.04 us -> 10.2 us
  transfers between devices with their start and end apart: 2 -> 2, of which waited for: 2 -> 1; matrix products, arithmetic and copies ran while one was open for 11% -> 11% of each run, Pallas kernels for 11% -> 17%
where the time goes in v3:
time: 433 us; the launch traced here: 425 us
  Pallas kernels  217 us (50%)
  waiting for transfers between devices  62.7 us (14%)
  local copies, waits for them, and re-layouts  48.9 us (11%)
  matrix products  47.3 us (11%)
  other arithmetic  33.3 us (8%)
  between operations  15.6 us (4%)
    pallas_call x8, Pallas kernels, sum_tensor(): pl.pallas_call(functools.partial(sum_tensor_kernel, pieces), out_shape=ja...  92.3 us
    psum x1, waiting for transfers between devices, layer_backward(): late, grad_out_weight = lax.psum((late, grad_out_weight), 'dp')  62.7 us
    pallas_call x2, Pallas kernels, scatter_dp(): pl.pallas_call(functools.partial(scatter_kernel, count), out_shape=jax.Sh...  57 us
    pallas_call x2, Pallas kernels, gather_dp(): pl.pallas_call(functools.partial(gather_kernel, count), out_shape=jax.Sha...  46.7 us
    pallas_call x2, Pallas kernels, swap_sections(): pl.pallas_call(functools.partial(swap_kernel, pieces), out_shape=jax.Shap...  20.8 us
    unnamed x159, local copies, waits for them, and re-layouts  10.2 us
  transfers between devices with their start and end apart: 2, of which 1 were waited for; matrix products, arithmetic and copies ran while one was open for 11% of the time, Pallas kernels for 17%

profile of v3, /device:TPU:0, one launch (start us, length us, event | category | flops | bytes accessed | tf_op | source)
XLA Modules:
  0.0 424.8 jit_solution(13521495941345882745)
XLA Ops:
  7.3 1.4 reduce.13
  15.9 24.4 %shard_map.220 = bf16[4,3,128,384]{3,2,1,0:T(8,128)(2,1)S(1)} custom-call(bf16[3,128,384]{2,1,0:T(8,128)(2,1)S(1)} %bitcast.207), custom_call_target="tpu_custom_call" | custom-call | tf_op jit(solution)/shard_map/pallas_call | solution.py:274
  40.2 2.0 copy.36
  42.2 2.5 reshape.291
  45.6 3.6 fusion.176
  49.2 2.3 fusion.64
  52.0 11.7 %shard_map.221 = f32[384,768]{1,0:T(8,128)S(1)} custom-call(f32[384,768]{1,0:T(8,128)S(1)} %fusion.112.x_ref), custom_call_target="tpu_custom_call" | custom-call | tf_op jit(solution)/shard_map/pallas_call | solution.py:132
  65.0 2.6 fusion.31.x_ref
  67.6 11.7 %shard_map.222 = f32[384,768]{1,0:T(8,128)S(1)} custom-call(f32[384,768]{1,0:T(8,128)S(1)} %fusion.31.x_ref), custom_call_target="tpu_custom_call" | custom-call | tf_op jit(solution)/shard_map/pallas_call | solution.py:132
  80.1 1.4 add_convert_fusion.4.x_ref
  81.5 10.4 %shard_map.223 = bf16[384,768]{1,0:T(8,128)(2,1)S(1)} custom-call(bf16[384,768]{1,0:T(8,128)(2,1)S(1)} %add_convert_fusion.4.x_ref), custom_call_target="tpu_custom_call" | custom-call | tf_op jit(solution)/shard_map/pallas_call | solution.py:188
  94.5 22.3 %shard_map.224 = bf16[4,3,128,384]{3,2,1,0:T(8,128)(2,1)S(1)} custom-call(bf16[3,128,384]{2,1,0:T(8,128)(2,1)S(1)} %bitcast.208), custom_call_target="tpu_custom_call" | custom-call | tf_op jit(solution)/shard_map/pallas_call | solution.py:274
  116.8 2.0 copy.42
  118.9 2.5 reshape.294
  121.4 4.0 fusion.179
  125.4 2.3 fusion.63
  129.0 10.8 %shard_map.225 = f32[384,768]{1,0:T(8,128)S(1)} custom-call(f32[384,768]{1,0:T(8,128)S(1)} %fusion.110.x_ref), custom_call_target="tpu_custom_call" | custom-call | tf_op jit(solution)/shard_map/pallas_call | solution.py:132
  141.9 1.7 convolution_add_fusion
  143.6 3.7 fusion.35.x_ref
  147.3 11.7 %shard_map.227 = f32[384,768]{1,0:T(8,128)S(1)} custom-call(f32[384,768]{1,0:T(8,128)S(1)} %fusion.35.x_ref), custom_call_target="tpu_custom_call" | custom-call | tf_op jit(solution)/shard_map/pallas_call | solution.py:132
  161.5 3.0 fusion.6
  170.3 20.1 %shard_map.228 = f32[3,128,384]{2,1,0:T(8,128)S(1)} custom-call(bf16[4,3,128,384]{3,2,1,0:T(8,128)(2,1)S(1)} %maximum_bitcast_fusion.x_ref), custom_call_target="tpu_custom_call" | custom-call | tf_op jit(solution)/shard_map/pallas_call | solution.py:355
  192.3 11.7 %shard_map.229 = f32[384,768]{1,0:T(8,128)S(1)} custom-call(f32[384,768]{1,0:T(8,128)S(1)} %fusion.96.x_ref), custom_call_target="tpu_custom_call" | custom-call | tf_op jit(solution)/shard_map/pallas_call | solution.py:132
  206.6 10.4 %shard_map.230 = bf16[384,768]{1,0:T(8,128)(2,1)S(1)} custom-call(bf16[384,768]{1,0:T(8,128)(2,1)S(1)} %add_convert_fusion.x_ref), custom_call_target="tpu_custom_call" | custom-call | tf_op jit(solution)/shard_map/pallas_call | solution.py:188
  217.0 2.0 fusion.183
  218.9 2.1 convolution_convert_fusion.1
  222.3 2.0 convolution_convert_fusion
  224.6 2.1 fusion.29.x_ref
  226.7 11.7 %shard_map.231 = f32[384,768]{1,0:T(8,128)S(1)} custom-call(f32[384,768]{1,0:T(8,128)S(1)} %fusion.33.x_ref), custom_call_target="tpu_custom_call" | custom-call | tf_op jit(solution)/shard_map/pallas_call | solution.py:132
  239.5 11.7 %shard_map.226 = f32[384,768]{1,0:T(8,128)S(1)} custom-call(f32[384,768]{1,0:T(8,128)S(1)} %fusion.29.x_ref), custom_call_target="tpu_custom_call" | custom-call | tf_op jit(solution)/shard_map/pallas_call | solution.py:132
  254.2 2.2 fusion.7
  256.9 2.0 multiply_reduce_fusion
  260.0 2.8 multiply_convert_fusion
  263.9 2.3 concatenate.43
  266.2 2.2 copy.58
  268.4 1.6 maximum_bitcast_fusion.1.x_ref
  270.0 36.9 %shard_map.232 = f32[3,128,384]{2,1,0:T(8,128)S(1)} custom-call(bf16[4,3,128,384]{3,2,1,0:T(8,128)(2,1)S(1)} %maximum_bitcast_fusion.1.x_ref), custom_call_target="tpu_custom_call" | custom-call | tf_op jit(solution)/shard_map/pallas_call | solution.py:355
  311.0 11.2 %shard_map.233 = f32[384,768]{1,0:T(8,128)S(1)} custom-call(f32[384,768]{1,0:T(8,128)S(1)} %fusion.103.x_ref), custom_call_target="tpu_custom_call" | custom-call | tf_op jit(solution)/shard_map/pallas_call | solution.py:132
  322.9 1.7 slice_reduce_fusion
  326.4 6.8 %concatenate.47 = bf16[5760]{0:T(1024)(128)(2,1)} concatenate(bf16[768]{0:T(1024)(128)(2,1)} %get-tuple-element.28, bf16[768]{0:T(1024)(128)(2,1)} %get-tuple-element.26, bf16[768]{0:T(1024)(128)(2,1)} %get-tuple-element.31, bf16[768]{0:T(1024)(128)(2,1)} %get-tuple-element.30, bf16[192]{0:T(256)(128)(2,1)} %reduce_sum.301, bf16[192]{0:T(256)(128)(2,1)} %slice_reduce_fusion, ...), dimensions={0} | concatenate | bytes 23040 | tf_op jit(solution)/shard_map/concatenate | solution.py:540
  333.1 1.4 convert_element_type.231
  334.5 1.5 copy.61
  336.1 2.0 convolution_convert_fusion.2
  340.8 2.7 add_add_fusion.4
  343.5 1.6 bitcast_convert_fusion.1
  345.2 1.6 bitcast_convert_fusion
  346.8 62.7 %all-reduce.5.cloned.1.call-done = (bf16[778,576]{0,1:T(8,128)(2,1)}, bf16[1,192,768]{2,1,0:T(8,128)(2,1)}) async-done(((bf16[778,576]{0,1:T(8,128)(2,1)}, bf16[1,192,768]{2,1,0:T(8,128)(2,1)}), (bf16[778,576]{0,1:T(8,128)(2,1)}, bf16[1,192,768]{2,1,0:T(8,128)(2,1)})) %all-reduce.5.cloned.1.call-update) | async-done | bytes 1191184 | tf_op jit(solution)/shard_map/psum | solution.py:558
  410.4 2.5 slice.154
  (267 shorter events, 51.8 us)
Async XLA Ops:
  7.2 57.8 %copy-start = (bf16[1,768,768]{2,1,0:T(8,128)(2,1)S(1)}, bf16[1,768,768]{2,1,0:T(8,128)(2,1)}, u32[]{:S(2)}) copy-start(bf16[1,768,768]{2,1,0:T(8,128)(2,1)} %param.23) | copy-start | bytes 3538948
  7.2 7.3 %copy-start.7 = (bf16[3,128,768]{2,1,0:T(8,128)(2,1)S(1)}, bf16[3,128,768]{2,1,0:T(8,128)(2,1)}, u32[]{:S(2)}) copy-start(bf16[3,128,768]{2,1,0:T(8,128)(2,1)} %param.13) | copy-start | bytes 1769476
  7.2 6.6 %copy-start.77 = (f32[1,2,192]{2,1,0:T(2,128)S(1)}, f32[1,2,192]{2,1,0:T(2,128)}, u32[]{:S(2)}) copy-start(f32[1,2,192]{2,1,0:T(2,128)} %param.18) | copy-start | bytes 4612
  7.2 6.6 %copy-start.72 = (f32[1,2,768]{2,1,0:T(2,128)S(1)}, f32[1,2,768]{2,1,0:T(2,128)}, u32[]{:S(2)}) copy-start(f32[1,2,768]{2,1,0:T(2,128)} %param.16) | copy-start | bytes 18436
  7.2 6.6 %copy-start.73 = (f32[1,2,768]{2,1,0:T(2,128)S(1)}, f32[1,2,768]{2,1,0:T(2,128)}, u32[]{:S(2)}) copy-start(f32[1,2,768]{2,1,0:T(2,128)} %param.15) | copy-start | bytes 18436
  7.2 333.5 %all-reduce.7.cloned.1.call-start = ((), (), s32[]{:S(2)}) async-start(), calls=%async_computation.1 | async-start | bytes 4718592 | tf_op jit(solution)/shard_map/psum | solution.py:487
  9.4 54.3 %copy-start.50 = (f32[768]{0:T(1024)}, f32[768]{0:T(1024)S(1)}, u32[]{:S(2)}) copy-start(f32[768]{0:T(1024)S(1)} %reduce.10) | copy-start | bytes 9220
  11.1 3.7 copy-start.12
  13.8 1.6 copy-start.67
  14.5 78.1 %copy-start.46 = (f32[768]{0:T(1024)}, f32[768]{0:T(1024)S(1)}, u32[]{:S(2)}) copy-start(f32[768]{0:T(1024)S(1)} %get-tuple-element.36) | copy-start | bytes 9220
  45.6 3.6 copy-start.45
  49.2 2.5 copy-start.23
  81.5 10.4 %copy-start.8 = (bf16[3,128,768]{2,1,0:T(8,128)(2,1)S(1)}, bf16[3,128,768]{2,1,0:T(8,128)(2,1)}, u32[]{:S(2)}) copy-start(bf16[3,128,768]{2,1,0:T(8,128)(2,1)} %param.13) | copy-start | bytes 1769476
  121.3 4.1 copy-start.27
  121.4 4.0 copy-start.34
  125.4 2.3 copy-start.62
  125.4 3.2 copy-start.24
  129.0 10.9 %copy-start.9 = (bf16[3,128,768]{2,1,0:T(8,128)(2,1)S(1)}, bf16[3,128,768]{2,1,0:T(8,128)(2,1)}, u32[]{:S(2)}) copy-start(bf16[3,128,768]{2,1,0:T(8,128)(2,1)} %param.13) | copy-start | bytes 1769476
  129.0 10.9 %copy-start.51 = (f32[768]{0:T(1024)S(1)}, f32[768]{0:T(1024)}, u32[]{:S(2)}) copy-start(f32[768]{0:T(1024)} %copy-done.50) | copy-start | bytes 9220
  140.1 19.5 %copy-start.4 = (f32[384,768]{1,0:T(8,128)}, f32[384,768]{1,0:T(8,128)S(1)}, u32[]{:S(2)}) copy-start(f32[384,768]{1,0:T(8,128)S(1)} %get-tuple-element.48) | copy-start | bytes 3538948
  140.1 1.7 copy-start.39
  140.2 1.7 copy-start.74
  140.2 1.7 copy-start.76
  141.9 1.8 copy-start.55
  161.5 3.0 copy-start.19
  161.5 3.0 copy-start.28
  192.3 11.7 %copy-start.2 = (f32[384,768]{1,0:T(8,128)S(1)}, f32[384,768]{1,0:T(8,128)}, u32[]{:S(2)}) copy-start(f32[384,768]{1,0:T(8,128)} %copy-done.1) | copy-start | bytes 3538948
  206.1 10.9 %copy-start.78 = (f32[384,768]{1,0:T(8,128)S(1)}, f32[384,768]{1,0:T(8,128)}, u32[]{:S(2)}) copy-start(f32[384,768]{1,0:T(8,128)} %convolution_add_fusion) | copy-start | bytes 3538948
  218.9 2.1 copy-start.40
  224.3 185.2 %all-reduce.5.cloned.1.call-start = ((), (), s32[]{:S(2)}) async-start(), calls=%async_computation | async-start | bytes 2654208 | tf_op jit(solution)/shard_map/psum | solution.py:558
  226.7 11.8 %copy-start.6 = (f32[384,768]{1,0:T(8,128)S(1)}, f32[384,768]{1,0:T(8,128)}, u32[]{:S(2)}) copy-start(f32[384,768]{1,0:T(8,128)} %copy-done.4) | copy-start | bytes 3538948
  226.7 11.7 %copy-start.58 = (f32[384]{0:T(512)S(1)}, f32[384]{0:T(512)}, u32[]{:S(2)}) copy-start(f32[384]{0:T(512)} %copy-done.55) | copy-start | bytes 4612
  239.5 11.7 %copy-start.49 = (f32[768]{0:T(1024)S(1)}, f32[768]{0:T(1024)}, u32[]{:S(2)}) copy-start(f32[768]{0:T(1024)} %copy-done.48) | copy-start | bytes 9220
  253.5 2.9 copy-start.10
  254.2 2.4 copy-start.20
  254.2 2.7 copy-start.29
  260.0 2.8 copy-start.36
  270.0 37.0 %copy-start.30 = (bf16[3,512,2,3,64]{1,4,3,2,0:T(8,128)(2,1)S(1)}, bf16[3,512,2,3,64]{1,4,3,2,0:T(8,128)(2,1)}, u32[]{:S(2)}) copy-start(bf16[3,512,2,3,64]{1,4,3,2,0:T(8,128)(2,1)} %copy-done.27) | copy-start | bytes 3538948
  307.0 2.6 copy-start.31
  307.0 3.3 copy-start.15
  311.0 13.5 %copy-start.3 = (f32[384,768]{1,0:T(8,128)S(1)}, f32[384,768]{1,0:T(8,128)}, u32[]{:S(2)}) copy-start(f32[384,768]{1,0:T(8,128)} %copy-done.1) | copy-start | bytes 3538948
  325.3 10.8 %copy-start.47 = (f32[768]{0:T(1024)S(1)}, f32[768]{0:T(1024)}, u32[]{:S(2)}) copy-start(f32[768]{0:T(1024)} %copy-done.46) | copy-start | bytes 9220
  336.1 2.0 copy-start.42
  338.1 1.6 copy-start.11
  338.1 1.6 copy-start.33
  340.8 2.7 copy-start.38
  343.5 1.7 copy-start.37
  410.4 4.7 %copy-start.44 = (bf16[1,192,768]{2,1,0:T(8,128)(2,1)S(1)}, bf16[1,192,768]{2,1,0:T(8,128)(2,1)}, u32[]{:S(2)}) copy-start(bf16[1,192,768]{2,1,0:T(8,128)(2,1)} %get-tuple-element.38) | copy-start | bytes 884740
  (33 other events, 34.2 us)
Sparse Core Ops, SparseCore 0:
  224.4 106.3 all-reduce.6
  340.9 68.5 all-reduce.4
